TPU v7x, 128 devices: a whole 4x4x4 slice. The times are simulated.
128 devices in a mesh: dp: 16 (over x, z_lo, core), mp: 8 (over z_hi, y).
Axes of the slice: x: 4, y: 4, z: 4 (z_hi: 2, z_lo: 2; z = z_hi * 2 + z_lo), core: 2. Of those that a mesh axis runs over, the one named last changes fastest.
Arguments:
- inputs: bfloat16 [4096, 6144], P('dp', 'mp'), may hold values from -26 to 26
- out_grad: bfloat16 [4096, 6144], P('dp', 'mp'), may hold values from -6 to 6
- attn_grad: bfloat16 [4096, 6144], P('dp', 'mp'), may hold values from -6 to 6
- hidden_grad: bfloat16 [4096, 12288], P('dp', 'mp'), may hold values from -6 to 6
- gain: float32 [6144], replicated, may hold values from 0.1 to 1.9
- w_in: bfloat16 [6144, 12288], P(None, 'mp'), may hold values from -0.078125 to 0.078125
Outputs:
- input_grad: bfloat16 [4096, 6144], P('dp', 'mp')
- weight_grad: float32 [6144, 12288], P('dp', 'mp')
- gain_grad: float32 [6144], P('mp')
All inputs are finite; a program needn't handle non-finite values.
Results may differ from a plain program's by a relative error of at most 0.02.
Values may be sent and summed in bfloat16 or wider, within the bound.
No kernel may reach another device: no remote copies, remote signals or barrier semaphores. Data moves between devices by JAX's collectives and lax.ppermute only.
A program may use at most 128 MiB of HBM per device.

v0:
```python
import jax
import jax.numpy as jnp
from jax import lax
from jax.sharding import PartitionSpec as P

epsilon = 1e-06


def gelu_slope(values):
    normal_cdf = 0.5 * (1.0 + lax.erf(values * 0.7071067811865476))
    normal_pdf = jnp.exp(-0.5 * values * values) * 0.3989422804014327
    return normal_cdf + values * normal_pdf


def local(inputs, out_grad, attn_grad, hidden_grad, gain, w_in):
    gathered = lax.all_gather(inputs, "mp", axis=1, tiled=True)
    own_width = inputs.shape[1]
    feature_offset = lax.axis_index("mp") * own_width
    floated = gathered.astype(jnp.float32)
    centred = floated - jnp.mean(floated, axis=1, keepdims=True)
    inv_scale = lax.rsqrt(jnp.mean(centred * centred, axis=1, keepdims=True) + epsilon)
    scaled = centred * inv_scale
    normed = (scaled * gain).astype(jnp.bfloat16)
    pre_act = jnp.dot(normed, w_in, preferred_element_type=jnp.float32)
    pre_grad = (hidden_grad.astype(jnp.float32) * gelu_slope(pre_act)).astype(jnp.bfloat16)
    weight_grad = lax.psum_scatter(
        lax.dot_general(
            normed, pre_grad, (((0,), (0,)), ((), ())), preferred_element_type=jnp.float32
        ).astype(jnp.bfloat16),
        "dp",
        scatter_dimension=0,
        tiled=True,
    ).astype(jnp.float32)
    input_term = lax.dot_general(
        pre_grad, w_in, (((1,), (1,)), ((), ())), preferred_element_type=jnp.float32
    )
    scaled_own = lax.dynamic_slice_in_dim(scaled, feature_offset, own_width, 1)
    summed = lax.psum(input_term.astype(jnp.bfloat16), "mp").astype(jnp.float32)
    branch_full = lax.all_gather(attn_grad, "mp", axis=1, tiled=True)
    dnorm_full = summed + branch_full.astype(jnp.float32)
    dxhat_full = dnorm_full * gain
    first_mean = jnp.mean(dxhat_full, axis=1, keepdims=True)
    second_mean = jnp.mean(dxhat_full * scaled, axis=1, keepdims=True)
    dnorm_own = lax.dynamic_slice_in_dim(dnorm_full, feature_offset, own_width, 1)
    dxhat_own = lax.dynamic_slice_in_dim(dxhat_full, feature_offset, own_width, 1)
    input_grad = (
        out_grad.astype(jnp.float32)
        + inv_scale * (dxhat_own - first_mean - scaled_own * second_mean)
    ).astype(jnp.bfloat16)
    gain_grad = lax.psum(jnp.sum(dnorm_own * scaled_own, axis=0), "dp")
    return (input_grad, weight_grad, gain_grad)


def solution(mesh):
    in_specs = (P("dp", "mp"), P("dp", "mp"), P("dp", "mp"), P("dp", "mp"), P(), P(None, "mp"))
    out_specs = (P("dp", "mp"), P("dp", "mp"), P("mp"))
    return jax.shard_map(local, mesh=mesh, in_specs=in_specs, out_specs=out_specs, check_vma=False)
```

profile of v0, /device:TPU:24, one launch (start us, length us, event | category | flops | bytes accessed | tf_op | source)
XLA Modules:
  0.0 446.2 jit_solution(10042306837678625135)
XLA Ops:
  7.2 0.0 all-gather.3.cloned.1.call-start
  7.2 0.7 all-gather.3.cloned.1.call-update
  7.9 0.0 all-gather.5.cloned.1.call-start
  7.9 0.0 copy-start.2
  8.0 0.7 all-gather.5.cloned.1.call-update
  8.6 0.0 all-reduce.2.cloned.1.call-start
  8.7 65.6 %all-gather.3.cloned.1.call-done = bf16[256,6144]{1,0:T(8,128)(2,1)} async-done(((bf16[256,768]{1,0:T(8,128)(2,1)}), bf16[256,6144]{1,0:T(8,128)(2,1)}) %all-gather.3.cloned.1.call-update) | async-done | bytes 3145744 | tf_op jit(solution)/shard_map/all_gather | solution.py:16
  74.3 2.5 convert_reduce_fusion
  76.8 0.3 copy-done
  77.1 1.0 fusion.2
  78.1 9.3 %fusion.13 = f32[256,1536]{1,0:T(8,128)S(1)} fusion(bf16[6144,1536]{1,0:T(8,128)(2,1)} %param.11, f32[6144]{0:T(1024)S(1)} %copy-done.2, bf16[256,6144]{1,0:T(8,128)(2,1)S(1)} %copy-done, f32[256]{0:T(256)S(1)} %add_rsqrt_fusion, f32[256]{0:T(256)S(1)} %broadcast_multiply_fusion.3), kind=kOutput, calls=%fused_computation.20 | convolution fusion | flops 4839702528 | bytes 23619584 | tf_op jit(solution)/shard_map/dot_general | solution.py:24
  87.4 1.1 copy-done.4
  88.6 10.8 %convolution_convert_fusion.1 = bf16[256,6144]{1,0:T(8,128)(2,1)} fusion(bf16[6144,1536]{1,0:T(8,128)(2,1)} %param.11, f32[256,1536]{1,0:T(8,128)S(1)} %fusion.13, bf16[256,1536]{1,0:T(8,128)(2,1)S(1)} %copy-done.3), kind=kOutput, calls=%fused_computation.3 | convolution fusion | flops 4837736448 | bytes 24379392 | tf_op jit(solution)/shard_map/dot_general | solution.py:34
  99.3 0.0 all-reduce.2.cloned.1.call-update
  99.4 0.0 reduce-scatter.2.cloned.1.call-start
  99.4 11.5 %convolution_convert_fusion = bf16[6144,1536]{1,0:T(8,128)(2,1)} fusion(f32[256,1536]{1,0:T(8,128)} %copy-done.4, bf16[256,1536]{1,0:T(8,128)(2,1)} %param.9, f32[6144]{0:T(1024)S(1)} %copy-done.2, bf16[256,6144]{1,0:T(8,128)(2,1)S(1)} %copy-done, f32[256]{0:T(256)S(1)} %add_rsqrt_fusion, f32[256]{0:T(256)S(1)} %broadcast_multiply_fusion.3), kind=kOutput, calls=%fused_computation | convolution fusion | flops 4853465088 | bytes 24406016 | tf_op jit(solution)/shard_map/dot_general | solution.py:27
  111.0 0.0 reduce-scatter.2.cloned.1.call-update
  111.0 26.4 %all-gather.5.cloned.1.call-done = bf16[256,6144]{1,0:T(8,128)(2,1)} async-done(((bf16[256,768]{1,0:T(8,128)(2,1)}), bf16[256,6144]{1,0:T(8,128)(2,1)}) %all-gather.5.cloned.1.call-update) | async-done | bytes 3145744 | tf_op jit(solution)/shard_map/all_gather | solution.py:39
  137.4 99.0 %all-reduce.2.cloned.1.call-done = bf16[256,6144]{1,0:T(8,128)(2,1)} async-done(((bf16[256,6144]{1,0:T(8,128)(2,1)}), bf16[256,6144]{1,0:T(8,128)(2,1)}) %all-reduce.2.cloned.1.call-update) | async-done | bytes 3145744 | tf_op jit(solution)/shard_map/psum | solution.py:38
  236.4 5.8 %fusion.36 = (f32[256]{0:T(256)S(1)}, f32[256]{0:T(256)S(1)}, f32[256,6144]{1,0:T(8,128)S(1)}, f32[256,6144]{1,0:T(8,128)S(1)}, f32[256,6144]{1,0:T(8,128)S(1)}) fusion(f32[256]{0:T(256)S(1)} %add_rsqrt_fusion, f32[256]{0:T(256)S(1)} %broadcast_multiply_fusion.3, bf16[256,6144]{1,0:T(8,128)(2,1)S(1)} %copy-done, f32[6144]{0:T(1024)} %param.10, ...), kind=kLoop, calls=%fused_computation.47 | loop fusion | flops 15728128 | bytes 28340224 | tf_op jit(solution)/shard_map/reduce_sum | solution.py:42
  242.2 1.0 multiply_reduce_fusion.1
  243.3 34.2 %psum.15 = f32[768]{0:T(1024)} all-reduce(f32[768]{0:T(1024)S(1)} %get-tuple-element.6), channel_id=1, replica_groups=mesh['dp'=16,'mp'=8] {'dp'}, use_global_device_ids=true, to_apply=%region_7.0 | all-reduce | flops 768 | bytes 6144 | tf_op jit(solution)/shard_map/psum | solution.py:50
  277.4 159.2 %reduce-scatter.2.cloned.1.call-done = bf16[384,1536]{1,0:T(8,128)(2,1)} async-done(((bf16[6144,1536]{1,0:T(8,128)(2,1)}), bf16[384,1536]{1,0:T(8,128)(2,1)}) %reduce-scatter.2.cloned.1.call-update) | async-done | bytes 1179664 | tf_op jit(solution)/shard_map/reduce_scatter | solution.py:26
  436.7 3.0 convert_element_type.43
  (10 shorter events, 0.0 us)
Async XLA Ops:
  7.2 67.1 %all-gather.3.cloned.1.call-start = ((), (), s32[]{:S(2)}) async-start(), calls=%async_computation.1 | async-start | bytes 3538944 | tf_op jit(solution)/shard_map/all_gather | solution.py:16
  7.9 129.5 %all-gather.5.cloned.1.call-start = ((), (), s32[]{:S(2)}) async-start(), calls=%async_computation.3 | async-start | bytes 3538944 | tf_op jit(solution)/shard_map/all_gather | solution.py:39
  7.9 70.2 %copy-start.2 = (f32[6144]{0:T(1024)S(1)}, f32[6144]{0:T(1024)}, u32[]{:S(2)}) copy-start(f32[6144]{0:T(1024)} %param.10) | copy-start | bytes 73732
  8.6 227.7 %all-reduce.2.cloned.1.call-start = ((), (), s32[]{:S(2)}) async-start(), calls=%async_computation.2 | async-start | bytes 6291456 | tf_op jit(solution)/shard_map/psum | solution.py:38
  74.3 2.8 copy-start
  78.1 10.4 %copy-start.3 = (bf16[256,1536]{1,0:T(8,128)(2,1)S(1)}, bf16[256,1536]{1,0:T(8,128)(2,1)}, u32[]{:S(2)}) copy-start(bf16[256,1536]{1,0:T(8,128)(2,1)} %param.9) | copy-start | bytes 2359300
  87.4 1.1 copy-start.4
  99.4 337.3 %reduce-scatter.2.cloned.1.call-start = ((), (), s32[]{:S(2)}) async-start(), calls=%async_computation.4 | async-start | bytes 20054016 | tf_op jit(solution)/shard_map/reduce_scatter | solution.py:26
  111.0 131.2 %copy-start.1 = (bf16[256,768]{1,0:T(8,128)(2,1)S(1)}, bf16[256,768]{1,0:T(8,128)(2,1)}, u32[]{:S(2)}) copy-start(bf16[256,768]{1,0:T(8,128)(2,1)} %param.7) | copy-start | bytes 1179652
Sparse Core Ops, SparseCore 0:
  10.3 63.9 all-gather.2
  76.6 60.7 all-gather.4
  139.9 96.4 all-reduce.1
  238.7 197.9 reduce-scatter.1
where the time goes:
time: 453 us; the launch traced here: 446 us
  waiting for transfers between devices  352 us (78%)
  blocking collectives  34.2 us (8%)
  matrix products  31.6 us (7%)
  between operations  13.8 us (3%)
  other arithmetic  13.3 us (3%)
    reduce_scatter x1, waiting for transfers between devices, local(): lax.psum_scatter(lax.dot_general(normed, pre_grad, (((0,), (0,)), ((), ()...  159 us
    psum x1, waiting for transfers between devices, local(): summed = lax.psum(input_term.astype(jnp.bfloat16), 'mp').astype(jnp.float32)  99 us
    all_gather x1, waiting for transfers between devices, local(): gathered = lax.all_gather(inputs, 'mp', axis=1, tiled=True)  65.6 us
    psum x1, blocking collectives, local(): gain_grad = lax.psum(jnp.sum(dnorm_own * scaled_own, axis=0), 'dp')  34.2 us
    all_gather x1, waiting for transfers between devices, local(): branch_full = lax.all_gather(attn_grad, 'mp', axis=1, tiled=True)  26.4 us
    dot_general x1, matrix products, local(): lax.dot_general(normed, pre_grad, (((0,), (0,)), ((), ())), preferred_ele...  11.5 us
    dot_general x1, matrix products, local(): lax.dot_general(pre_grad, w_in, (((1,), (1,)), ((), ())), preferred_eleme...  10.8 us
    dot_general x1, matrix products, local(): pre_act = jnp.dot(normed, w_in, preferred_element_type=jnp.float32)  9.27 us
  transfers between devices with their start and end apart: 4, of which 4 were waited for; matrix products, arithmetic and copies ran while one was open for 9% of the time, Pallas kernels for 0%

commit v1 on v0

v1 whole, which is shorter than its diff:
```python
import jax
import jax.numpy as jnp
from jax import lax
from jax.sharding import Mesh, PartitionSpec as P

epsilon = 1e-06
DP = ("x", "zl", "c")
MP = ("zh", "y")
f32 = jnp.float32
bf16 = jnp.bfloat16


def gelu_slope(values):
    normal_cdf = 0.5 * (1.0 + lax.erf(values * 0.7071067811865476))
    normal_pdf = jnp.exp(-0.5 * values * values) * 0.3989422804014327
    return normal_cdf + values * normal_pdf


def shift(value, axis, step, size):
    return lax.ppermute(value, axis, [(i, (i + step) % size) for i in range(size)])


def columns(value, index, width):
    return lax.dynamic_slice_in_dim(value, index * width, width, 1)


def local(inputs, out_grad, attn_grad, hidden_grad, gain, w_in):
    own = inputs.shape[1]
    x, zl, c = (lax.axis_index(name) for name in DP)
    zh, y = (lax.axis_index(name) for name in MP)

    def block(dz, dy):
        return (zh ^ dz) * 4 + (y + dy) % 4

    parts = {(0, 0): inputs}
    parts[1, 0] = shift(inputs, "zh", 1, 2)
    parts[0, 3] = shift(inputs, "y", 1, 4)
    parts[0, 1] = shift(inputs, "y", 3, 4)
    parts[0, 2] = shift(inputs, "y", 2, 4)
    parts[1, 3] = shift(parts[1, 0], "y", 1, 4)
    parts[1, 1] = shift(parts[1, 0], "y", 3, 4)
    parts[1, 2] = shift(parts[0, 2], "zh", 1, 2)
    gathered = jnp.zeros((inputs.shape[0], own * 8), bf16)
    for (dz, dy), part in parts.items():
        gathered = lax.dynamic_update_slice_in_dim(gathered, part, block(dz, dy) * own, 1)
    floated = gathered.astype(f32)
    mean = jnp.mean(floated, axis=1, keepdims=True)
    centred = floated - mean
    inv_scale = lax.rsqrt(jnp.mean(centred * centred, axis=1, keepdims=True) + epsilon)
    scaled = centred * inv_scale
    normed = (scaled * gain).astype(bf16)

    wide = 2 * own
    normed_x = [columns(normed, x, wide)]
    for step in (1, 2, 3):
        normed_x.append(shift(columns(normed, (x + step) % 4, wide), "x", step, 4))

    pre_act = jnp.dot(normed, w_in, preferred_element_type=f32)
    pre_grad = (hidden_grad.astype(f32) * gelu_slope(pre_act)).astype(bf16)

    grads_x = [pre_grad] + [shift(pre_grad, "x", step, 4) for step in (1, 2, 3)]

    term = lax.dot_general(pre_grad, w_in, (((1,), (1,)), ((), ())), preferred_element_type=f32).astype(bf16)

    def piece(dz, dy):
        return columns(term, block(dz, dy), own)

    got_z = shift(piece(1, 2), "zh", 1, 2)
    got_p = shift(piece(1, 1), "y", 1, 4)
    got_m = shift(piece(1, 3), "y", 3, 4)
    near_p = shift(piece(0, 1), "y", 1, 4)
    near_m = shift(piece(0, 3), "y", 3, 4)
    far = shift((piece(0, 2).astype(f32) + got_z.astype(f32)).astype(bf16), "y", 2, 4)
    across = shift(
        (piece(1, 0).astype(f32) + got_p.astype(f32) + got_m.astype(f32)).astype(bf16), "zh", 1, 2
    )

    scaled_own = columns(scaled, block(0, 0), own)
    gain_own = lax.dynamic_slice_in_dim(gain, block(0, 0) * own, own, 0)
    attn = attn_grad.astype(f32)
    weighted = term.astype(f32) * gain
    sums = jnp.stack(
        [
            jnp.sum(weighted, axis=1) + jnp.sum(attn * gain_own, axis=1),
            jnp.sum(weighted * scaled, axis=1) + jnp.sum(attn * gain_own * scaled_own, axis=1),
        ]
    )
    sums = sums + shift(sums, "y", 1, 4) + shift(sums, "y", 2, 4) + shift(sums, "y", 3, 4)
    sums = (sums + shift(sums, "zh", 1, 2)) * (1.0 / (own * 8))
    first_mean, second_mean = sums[0][:, None], sums[1][:, None]

    normed_all = jnp.concatenate(normed_x, 0)
    grads_all = jnp.concatenate(grads_x, 0)
    rows = wide // 4

    def weight_part(dzl, dc):
        left = columns(normed_all, (zl ^ dzl) * 2 + (c ^ dc), rows)
        return lax.dot_general(left, grads_all, (((0,), (0,)), ((), ())), preferred_element_type=f32)

    sent = shift(weight_part(1, 1).astype(bf16), "c", 1, 2)
    sent = shift((weight_part(1, 0) + sent.astype(f32)).astype(bf16), "zl", 1, 2)
    other = shift(weight_part(0, 1).astype(bf16), "c", 1, 2)
    weight_grad = weight_part(0, 0) + other.astype(f32) + sent.astype(f32)

    dnorm = attn + piece(0, 0).astype(f32)
    for got in (near_p, near_m, far, across):
        dnorm = dnorm + got.astype(f32)
    dxhat = dnorm * gain_own
    input_grad = (
        out_grad.astype(f32) + inv_scale * (dxhat - first_mean - scaled_own * second_mean)
    ).astype(bf16)
    gain_grad = jnp.sum(dnorm * scaled_own, axis=0)
    gain_grad = gain_grad + shift(gain_grad, "c", 1, 2)
    gain_grad = gain_grad + shift(gain_grad, "zl", 1, 2)
    gain_grad = (
        gain_grad + shift(gain_grad, "x", 1, 4) + shift(gain_grad, "x", 2, 4) + shift(gain_grad, "x", 3, 4)
    )
    return (input_grad, weight_grad, gain_grad)


def solution(mesh):
    fine = Mesh(mesh.devices.reshape(4, 2, 2, 2, 4), DP + MP)
    both = P(DP, MP)
    in_specs = (both, both, both, both, P(), P(None, MP))
    out_specs = (both, both, P(MP))
    return jax.shard_map(local, mesh=fine, in_specs=in_specs, out_specs=out_specs, check_vma=False)
```

time: 453 us -> 213 us (0.47); the launches traced: 446 us -> 213 us
  waiting for transfers between devices: 352 us -> 110 us
  starting transfers between devices: 0.16 us -> 39.3 us
  blocking collectives: 34.2 us -> 0 us
  between operations: 13.8 us -> 0.87 us
  local copies, waits for them, and re-layouts: 1.44 us -> 9.76 us
  matrix products: 31.6 us -> 39.1 us
    reduce_scatter x1 -> x0, waiting for transfers between devices: 159 us -> none  [local(): lax.psum_scatter(lax.dot_general(normed, pre_grad, (((0,), (0,)), ((), ()...]
    ppermute x0 -> x32, waiting for transfers between devices: none -> 110 us  [shift(): lax.ppermute(value, axis, [(i, (i + step) % size) for i in range(size)])]
    psum x1 -> x0, waiting for transfers between devices: 99 us -> none  [local(): summed = lax.psum(input_term.astype(jnp.bfloat16), 'mp').astype(jnp.float32)]
    all_gather x2 -> x0, waiting for transfers between devices: 92 us -> none  [the longest x1 65.6 us: local(): gathered = lax.all_gather(inputs, 'mp', axis=1, tiled=True)]
    ppermute x0 -> x32, starting transfers between devices: none -> 39.3 us  [shift(): lax.ppermute(value, axis, [(i, (i + step) % size) for i in range(size)])]
    psum x1 -> x0, blocking collectives: 34.2 us -> none  [local(): gain_grad = lax.psum(jnp.sum(dnorm_own * scaled_own, axis=0), 'dp')]
    reduce_sum x3 -> x2, other arithmetic: 9.39 us -> 2.67 us  [the longest x1 2.16 us: local(): gain_grad = jnp.sum(dnorm * scaled_own, axis=0)]
    dot_general x2 -> x5, matrix products: 20.8 us -> 26 us  [the longest x4 19.1 us: weight_part(): lax.dot_general(left, grads_all, (((0,), (0,)), ((), ())), preferred_elem...]
  transfers between devices with their start and end apart: 4 -> 32, of which waited for: 4 -> 15; matrix products, arithmetic and copies ran while one was open for 9% -> 24% of each run, Pallas kernels for 0% -> 0%
where the time goes in v1:
time: 213 us
  waiting for transfers between devices  110 us (52%)
  starting transfers between devices  39.3 us (18%)
  matrix products  39.1 us (18%)
  other arithmetic  13.6 us (6%)
  local copies, waits for them, and re-layouts  9.76 us (5%)
    ppermute x32, waiting for transfers between devices, shift(): lax.ppermute(value, axis, [(i, (i + step) % size) for i in range(size)])  110 us
    ppermute x32, starting transfers between devices, shift(): lax.ppermute(value, axis, [(i, (i + step) % size) for i in range(size)])  39.3 us
    dot_general x4, matrix products, weight_part(): lax.dot_general(left, grads_all, (((0,), (0,)), ((), ())), preferred_elem...  19.1 us
    dot_general x1, matrix products, local(): lax.dot_general(pre_grad, w_in, (((1,), (1,)), ((), ())), preferred_eleme...  13.1 us
    dot_general x1, matrix products, local(): pre_act = jnp.dot(normed, w_in, preferred_element_type=f32)  6.9 us
    dynamic_update_slice x8, local copies, waits for them, and re-layouts, local(): lax.dynamic_update_slice_in_dim(gathered, part, block(dz, dy) * own, 1)  4.31 us
  transfers between devices with their start and end apart: 32, of which 15 were waited for; matrix products, arithmetic and copies ran while one was open for 24% of the time, Pallas kernels for 0%

profile of v1, /device:TPU:24, one launch (start us, length us, event | category | flops | bytes accessed | tf_op | source)
XLA Modules:
  0.0 212.9 jit_solution(13941942658132090028)
XLA Ops:
  0.6 4.0 %collective-permute-start = (bf16[256,768]{1,0:T(8,128)(2,1)}, bf16[256,768]{1,0:T(8,128)(2,1)}, u32[]{:S(2)}, u32[]{:S(2)}) collective-permute-start(bf16[256,768]{1,0:T(8,128)(2,1)} %param.6), channel_id=1, source_target_pairs={{0,4},{4,0},{1,5},{5,1},{2,6},{6,2},{3,7},{7,3},{8,12},{12,8},{9,1... | collective-permute-start | bytes 1179656 | tf_op jit(solution)/shard_map/ppermute | solution.py:20
  8.4 5.6 %collective-permute-done = bf16[256,768]{1,0:T(8,128)(2,1)} collective-permute-done((bf16[256,768]{1,0:T(8,128)(2,1)}, bf16[256,768]{1,0:T(8,128)(2,1)}, u32[]{:S(2)}, u32[]{:S(2)}) %collective-permute-start) | collective-permute-done | bytes 393248 | tf_op jit(solution)/shard_map/ppermute | solution.py:20
  21.6 2.9 %collective-permute-done.1 = bf16[256,768]{1,0:T(8,128)(2,1)} collective-permute-done((bf16[256,768]{1,0:T(8,128)(2,1)}, bf16[256,768]{1,0:T(8,128)(2,1)}, u32[]{:S(2)}, u32[]{:S(2)}) %collective-permute-start.1) | collective-permute-done | bytes 393248 | tf_op jit(solution)/shard_map/ppermute | solution.py:20
  27.6 3.7 %collective-permute-done.4 = bf16[256,768]{1,0:T(8,128)(2,1)S(1)} collective-permute-done((bf16[256,768]{1,0:T(8,128)(2,1)}, bf16[256,768]{1,0:T(8,128)(2,1)S(1)}, u32[]{:S(2)}, u32[]{:S(2)}) %collective-permute-start.4) | collective-permute-done | bytes 393248 | tf_op jit(solution)/shard_map/ppermute | solution.py:20
  38.3 2.8 %collective-permute-start.20 = (bf16[256,1536]{1,0:T(8,128)(2,1)S(1)}, bf16[256,1536]{1,0:T(8,128)(2,1)}, u32[]{:S(2)}, u32[]{:S(2)}) collective-permute-start(bf16[256,1536]{1,0:T(8,128)(2,1)S(1)} %get-tuple-element.10), channel_id=1, source_target_pairs={{0,96},{32,0},{64,32},{96,64},{1,97},{33,1},{65,33},{97,65},{2,98}... | collective-permute-start | bytes 2359304 | tf_op jit(solution)/shard_map/ppermute | solution.py:20
  41.3 6.9 %fusion.11 = (bf16[256,1536]{1,0:T(8,128)(2,1)}, f32[256,1536]{1,0:T(8,128)}) fusion(bf16[256,1536]{1,0:T(8,128)(2,1)S(1)} %copy-done.8, bf16[256,6144]{1,0:T(8,128)(2,1)S(1)} %multiply_convert_fusion, bf16[6144,1536]{1,0:T(8,128)(2,1)S(1)} %copy-done.7), kind=kOutput, calls=%fused_computation.24 | convolution fusion | flops 4836163584 | bytes 25165824 | tf_op jit(solution)/shard_map/dot_general | solution.py:58
  48.2 2.8 %collective-permute-start.23 = (bf16[256,1536]{1,0:T(8,128)(2,1)}, bf16[256,1536]{1,0:T(8,128)(2,1)}, u32[]{:S(2)}, u32[]{:S(2)}) collective-permute-start(bf16[256,1536]{1,0:T(8,128)(2,1)} %get-tuple-element.23), channel_id=1, source_target_pairs={{0,96},{32,0},{64,32},{96,64},{1,97},{33,1},{65,33},{97,65},{2,98}... | collective-permute-start | bytes 2359304 | tf_op jit(solution)/shard_map/ppermute | solution.py:20
  54.5 4.5 %collective-permute-done.20 = bf16[256,1536]{1,0:T(8,128)(2,1)} collective-permute-done((bf16[256,1536]{1,0:T(8,128)(2,1)S(1)}, bf16[256,1536]{1,0:T(8,128)(2,1)}, u32[]{:S(2)}, u32[]{:S(2)}) %collective-permute-start.20) | collective-permute-done | bytes 786464 | tf_op jit(solution)/shard_map/ppermute | solution.py:20
  60.3 13.1 %fusion.3 = (f32[256]{0:T(256)S(1)}, f32[256]{0:T(256)}, f32[256,6144]{1,0:T(8,128)}, bf16[256,6144]{1,0:T(8,128)(2,1)}) fusion(f32[6144]{0:T(1024)S(1)} %copy-done.6, f32[256]{0:T(256)S(1)} %add_rsqrt_fusion, f32[256]{0:T(256)S(1)} %broadcast_multiply_fusion, bf16[256,6144]{1,0:T(8,128)(2,1)S(1)} %constant_dynamic-update-slice_fusion, ...), kind=kOutput, calls=%fused_computation.8 | convolution fusion | flops 4850319360 | bytes 33845248 | tf_op jit(solution)/shard_map/dot_general | solution.py:63
  73.4 2.5 %constant_dynamic-slice_fusion.8 = (bf16[256,768]{1,0:T(8,128)(2,1)}, bf16[256,768]{1,0:T(8,128)(2,1)S(1)}, bf16[256,768]{1,0:T(8,128)(2,1)S(1)}, bf16[256,768]{1,0:T(8,128)(2,1)S(1)}, bf16[256,768]{1,0:T(8,128)(2,1)}) fusion(bf16[256,6144]{1,0:T(8,128)(2,1)} %get-tuple-element.22, s32[]{:T(128)S(6)} %select_n.123, s32[]{:T(128)S(6)} %select_n.126, ...), kind=kLoop, calls=%fused_computation.60 | loop fusion | bytes 3932180 | tf_op jit(solution)/shard_map/dynamic_slice | solution.py:24
  75.9 31.1 %collective-permute-done.19 = bf16[256,1536]{1,0:T(8,128)(2,1)} collective-permute-done((bf16[256,1536]{1,0:T(8,128)(2,1)}, bf16[256,1536]{1,0:T(8,128)(2,1)}, u32[]{:S(2)}, u32[]{:S(2)}) %collective-permute-start.19) | collective-permute-done | bytes 786464 | tf_op jit(solution)/shard_map/ppermute | solution.py:20
  107.7 14.8 %collective-permute-done.18 = bf16[256,1536]{1,0:T(8,128)(2,1)} collective-permute-done((bf16[256,1536]{1,0:T(8,128)(2,1)}, bf16[256,1536]{1,0:T(8,128)(2,1)}, u32[]{:S(2)}, u32[]{:S(2)}) %collective-permute-start.18) | collective-permute-done | bytes 786464 | tf_op jit(solution)/shard_map/ppermute | solution.py:20
  124.3 3.3 %collective-permute-start.11 = (bf16[256,768]{1,0:T(8,128)(2,1)S(1)}, bf16[256,768]{1,0:T(8,128)(2,1)S(1)}, u32[]{:S(2)}, u32[]{:S(2)}) collective-permute-start(bf16[256,768]{1,0:T(8,128)(2,1)S(1)} %get-tuple-element.15), channel_id=1, source_target_pairs={{0,1},{1,2},{2,3},{3,0},{4,5},{5,6},{6,7},{7,4},{8,9},{9,10},{10,1... | collective-permute-start | bytes 1179656 | tf_op jit(solution)/shard_map/ppermute | solution.py:20
  128.0 4.4 %convolution_convert_fusion.1 = bf16[384,1536]{1,0:T(8,128)(2,1)} fusion(bf16[1024,1536]{1,0:T(8,128)(2,1)S(1)} %pad_maximum_fusion, s32[]{:T(128)S(6)} %select_n.139, bf16[256,1536]{1,0:T(8,128)(2,1)} %collective-permute-done.23, bf16[256,1536]{1,0:T(8,128)(2,1)} %collective-permute-done.22, bf16[256,1536]{1,0:T(8,128)(2,1)} %collective-permute-done.21, ...), kind=kOutput, calls=%fused_computation.16 | convolution fusion | flops 1221132288 | bytes 5111812 | tf_op jit(solution)/shard_map/dot_general | solution.py:98
  132.4 3.3 %collective-permute-done.12 = bf16[256,768]{1,0:T(8,128)(2,1)S(1)} collective-permute-done((bf16[256,768]{1,0:T(8,128)(2,1)S(1)}, bf16[256,768]{1,0:T(8,128)(2,1)S(1)}, u32[]{:S(2)}, u32[]{:S(2)}) %collective-permute-start.12) | collective-permute-done | bytes 393248 | tf_op jit(solution)/shard_map/ppermute | solution.py:20
  135.9 3.7 %collective-permute-done.9 = bf16[256,768]{1,0:T(8,128)(2,1)S(1)} collective-permute-done((bf16[256,768]{1,0:T(8,128)(2,1)S(1)}, bf16[256,768]{1,0:T(8,128)(2,1)S(1)}, u32[]{:S(2)}, u32[]{:S(2)}) %collective-permute-start.9) | collective-permute-done | bytes 393248 | tf_op jit(solution)/shard_map/ppermute | solution.py:20
  143.3 8.8 %collective-permute-done.10 = bf16[256,768]{1,0:T(8,128)(2,1)} collective-permute-done((bf16[256,768]{1,0:T(8,128)(2,1)}, bf16[256,768]{1,0:T(8,128)(2,1)}, u32[]{:S(2)}, u32[]{:S(2)}) %collective-permute-start.10) | collective-permute-done | bytes 393248 | tf_op jit(solution)/shard_map/ppermute | solution.py:20
  155.0 3.3 %collective-permute-start.15 = (f32[2,256]{1,0:T(2,128)S(1)}, f32[2,256]{1,0:T(2,128)S(1)}, u32[]{:S(2)}, u32[]{:S(2)}) collective-permute-start(f32[2,256]{1,0:T(2,128)S(1)} %pad_maximum_fusion.2), channel_id=1, source_target_pairs={{0,2},{1,3},{2,0},{3,1},{4,6},{5,7},{6,4},{7,5},{8,10},{9,11},{10,... | collective-permute-start | bytes 6152 | tf_op jit(solution)/shard_map/ppermute | solution.py:20
  158.3 3.2 %collective-permute-start.14 = (f32[2,256]{1,0:T(2,128)S(1)}, f32[2,256]{1,0:T(2,128)S(1)}, u32[]{:S(2)}, u32[]{:S(2)}) collective-permute-start(f32[2,256]{1,0:T(2,128)S(1)} %pad_maximum_fusion.2), channel_id=1, source_target_pairs={{0,1},{1,2},{2,3},{3,0},{4,5},{5,6},{6,7},{7,4},{8,9},{9,10},{10,1... | collective-permute-start | bytes 6152 | tf_op jit(solution)/shard_map/ppermute | solution.py:20
  161.6 4.3 %convolution_convert_fusion.2 = bf16[384,1536]{1,0:T(8,128)(2,1)} fusion(bf16[1024,1536]{1,0:T(8,128)(2,1)S(1)} %copy-done.2, s32[]{:T(128)S(6)} %select_n.137, bf16[256,1536]{1,0:T(8,128)(2,1)} %collective-permute-done.23, bf16[256,1536]{1,0:T(8,128)(2,1)} %collective-permute-done.22, bf16[256,1536]{1,0:T(8,128)(2,1)} %collective-permute-done.21, ...), kind=kOutput, calls=%fused_computation.17 | convolution fusion | flops 1221132288 | bytes 5111812 | tf_op jit(solution)/shard_map/dot_general | solution.py:98
  166.4 4.7 %fusion.5 = bf16[384,1536]{1,0:T(8,128)(2,1)} fusion(bf16[384,1536]{1,0:T(8,128)(2,1)} %collective-permute-done.25, bf16[1024,1536]{1,0:T(8,128)(2,1)S(1)} %copy-done.2, s32[]{:T(128)S(6)} %select_n.138, bf16[256,1536]{1,0:T(8,128)(2,1)} %collective-permute-done.23, bf16[256,1536]{1,0:T(8,128)(2,1)} %collective-permute-done.22, ...), kind=kOutput, calls=%fused_computation.15 | convolution fusion | flops 1222311936 | bytes 6291460 | tf_op jit(solution)/shard_map/dot_general | solution.py:98
  174.0 25.5 %collective-permute-done.17 = f32[2,256]{1,0:T(2,128)} collective-permute-done((f32[2,256]{1,0:T(2,128)S(1)}, f32[2,256]{1,0:T(2,128)}, u32[]{:S(2)}, u32[]{:S(2)}) %collective-permute-start.17) | collective-permute-done | bytes 2080 | tf_op jit(solution)/shard_map/ppermute | solution.py:20
  202.5 2.9 %add_convert_fusion = bf16[256,768]{1,0:T(8,128)(2,1)} fusion(bf16[256,768]{1,0:T(8,128)(2,1)} %param.7, f32[256,6144]{1,0:T(8,128)} %get-tuple-element.8, s32[]{:T(128)S(6)} %select_n.118, f32[256]{0:T(256)S(1)} %bitcast.12, f32[256]{0:T(256)S(1)} %bitcast.11, f32[768]{0:T(1024)S(1)} %dynamic_slice.62, f32[256]{0:T(256)S(1)} %add_rsqrt_fusion, ...), kind=kLoop, calls=%fused_computation.40 | loop fusion | flops 3735552 | bytes 3938308 | tf_op jit(solution)/shard_map/convert_element_type | solution.py:111
  207.2 5.7 %fusion.4 = f32[384,1536]{1,0:T(8,128)} fusion(bf16[384,1536]{1,0:T(8,128)(2,1)} %collective-permute-done.26, bf16[384,1536]{1,0:T(8,128)(2,1)} %collective-permute-done.24, bf16[1024,1536]{1,0:T(8,128)(2,1)} %copy-done.1, s32[]{:T(128)S(6)} %select_n.136, bf16[256,1536]{1,0:T(8,128)(2,1)} %collective-permute-done.23, ...), kind=kOutput, calls=%fused_computation.14 | convolution fusion | flops 1222901760 | bytes 8650756 | tf_op jit(solution)/shard_map/dot_general | solution.py:98
  (94 shorter events, 44.1 us)
Async XLA Ops:
  0.6 13.4 %collective-permute-start = (bf16[256,768]{1,0:T(8,128)(2,1)}, bf16[256,768]{1,0:T(8,128)(2,1)}, u32[]{:S(2)}, u32[]{:S(2)}) collective-permute-start(bf16[256,768]{1,0:T(8,128)(2,1)} %param.6), channel_id=1, source_target_pairs={{0,4},{4,0},{1,5},{5,1},{2,6},{6,2},{3,7},{7,3},{8,12},{12,8},{9,1... | collective-permute-start | bytes 1179656 | tf_op jit(solution)/shard_map/ppermute | solution.py:20
  4.6 13.9 %collective-permute-start.3 = (bf16[256,768]{1,0:T(8,128)(2,1)}, bf16[256,768]{1,0:T(8,128)(2,1)}, u32[]{:S(2)}, u32[]{:S(2)}) collective-permute-start(bf16[256,768]{1,0:T(8,128)(2,1)} %param.6), channel_id=1, source_target_pairs={{0,2},{1,3},{2,0},{3,1},{4,6},{5,7},{6,4},{7,5},{8,10},{9,11},{10,... | collective-permute-start | bytes 1179656 | tf_op jit(solution)/shard_map/ppermute | solution.py:20
  5.8 18.6 %collective-permute-start.1 = (bf16[256,768]{1,0:T(8,128)(2,1)}, bf16[256,768]{1,0:T(8,128)(2,1)}, u32[]{:S(2)}, u32[]{:S(2)}) collective-permute-start(bf16[256,768]{1,0:T(8,128)(2,1)} %param.6), channel_id=1, source_target_pairs={{0,1},{1,2},{2,3},{3,0},{4,5},{5,6},{6,7},{7,4},{8,9},{9,10},{10,1... | collective-permute-start | bytes 1179656 | tf_op jit(solution)/shard_map/ppermute | solution.py:20
  8.0 17.5 %collective-permute-start.2 = (bf16[256,768]{1,0:T(8,128)(2,1)}, bf16[256,768]{1,0:T(8,128)(2,1)}, u32[]{:S(2)}, u32[]{:S(2)}) collective-permute-start(bf16[256,768]{1,0:T(8,128)(2,1)} %param.6), channel_id=1, source_target_pairs={{0,3},{1,0},{2,1},{3,2},{4,7},{5,4},{6,5},{7,6},{8,11},{9,8},{10,9... | collective-permute-start | bytes 1179656 | tf_op jit(solution)/shard_map/ppermute | solution.py:20
  14.0 19.7 %collective-permute-start.5 = (bf16[256,768]{1,0:T(8,128)(2,1)}, bf16[256,768]{1,0:T(8,128)(2,1)S(1)}, u32[]{:S(2)}, u32[]{:S(2)}) collective-permute-start(bf16[256,768]{1,0:T(8,128)(2,1)} %collective-permute-done), channel_id=1, source_target_pairs={{0,3},{1,0},{2,1},{3,2},{4,7},{5,4},{6,5},{7,6},{8,11},{9,8},{10,9... | collective-permute-start | bytes 1179656 | tf_op jit(solution)/shard_map/ppermute | solution.py:20
  14.8 16.6 %collective-permute-start.4 = (bf16[256,768]{1,0:T(8,128)(2,1)}, bf16[256,768]{1,0:T(8,128)(2,1)S(1)}, u32[]{:S(2)}, u32[]{:S(2)}) collective-permute-start(bf16[256,768]{1,0:T(8,128)(2,1)} %collective-permute-done), channel_id=1, source_target_pairs={{0,1},{1,2},{2,3},{3,0},{4,5},{5,6},{6,7},{7,4},{8,9},{9,10},{10,1... | collective-permute-start | bytes 1179656 | tf_op jit(solution)/shard_map/ppermute | solution.py:20
  18.5 15.3 %collective-permute-start.6 = (bf16[256,768]{1,0:T(8,128)(2,1)}, bf16[256,768]{1,0:T(8,128)(2,1)S(1)}, u32[]{:S(2)}, u32[]{:S(2)}) collective-permute-start(bf16[256,768]{1,0:T(8,128)(2,1)} %collective-permute-done.3), channel_id=1, source_target_pairs={{0,4},{4,0},{1,5},{5,1},{2,6},{6,2},{3,7},{7,3},{8,12},{12,8},{9,1... | collective-permute-start | bytes 1179656 | tf_op jit(solution)/shard_map/ppermute | solution.py:20
  38.3 20.7 %collective-permute-start.20 = (bf16[256,1536]{1,0:T(8,128)(2,1)S(1)}, bf16[256,1536]{1,0:T(8,128)(2,1)}, u32[]{:S(2)}, u32[]{:S(2)}) collective-permute-start(bf16[256,1536]{1,0:T(8,128)(2,1)S(1)} %get-tuple-element.10), channel_id=1, source_target_pairs={{0,96},{32,0},{64,32},{96,64},{1,97},{33,1},{65,33},{97,65},{2,98}... | collective-permute-start | bytes 2359304 | tf_op jit(solution)/shard_map/ppermute | solution.py:20
  48.2 76.1 %collective-permute-start.23 = (bf16[256,1536]{1,0:T(8,128)(2,1)}, bf16[256,1536]{1,0:T(8,128)(2,1)}, u32[]{:S(2)}, u32[]{:S(2)}) collective-permute-start(bf16[256,1536]{1,0:T(8,128)(2,1)} %get-tuple-element.23), channel_id=1, source_target_pairs={{0,96},{32,0},{64,32},{96,64},{1,97},{33,1},{65,33},{97,65},{2,98}... | collective-permute-start | bytes 2359304 | tf_op jit(solution)/shard_map/ppermute | solution.py:20
  51.0 76.6 %collective-permute-start.22 = (bf16[256,1536]{1,0:T(8,128)(2,1)}, bf16[256,1536]{1,0:T(8,128)(2,1)}, u32[]{:S(2)}, u32[]{:S(2)}) collective-permute-start(bf16[256,1536]{1,0:T(8,128)(2,1)} %get-tuple-element.23), channel_id=1, source_target_pairs={{0,64},{32,96},{64,0},{96,32},{1,65},{33,97},{65,1},{97,33},{2,66}... | collective-permute-start | bytes 2359304 | tf_op jit(solution)/shard_map/ppermute | solution.py:20
  51.8 76.2 %collective-permute-start.21 = (bf16[256,1536]{1,0:T(8,128)(2,1)}, bf16[256,1536]{1,0:T(8,128)(2,1)}, u32[]{:S(2)}, u32[]{:S(2)}) collective-permute-start(bf16[256,1536]{1,0:T(8,128)(2,1)} %get-tuple-element.23), channel_id=1, source_target_pairs={{0,32},{32,64},{64,96},{96,0},{1,33},{33,65},{65,97},{97,1},{2,34}... | collective-permute-start | bytes 2359304 | tf_op jit(solution)/shard_map/ppermute | solution.py:20
  52.7 54.4 %collective-permute-start.19 = (bf16[256,1536]{1,0:T(8,128)(2,1)}, bf16[256,1536]{1,0:T(8,128)(2,1)}, u32[]{:S(2)}, u32[]{:S(2)}) collective-permute-start(bf16[256,1536]{1,0:T(8,128)(2,1)} %get-tuple-element.11), channel_id=1, source_target_pairs={{0,64},{32,96},{64,0},{96,32},{1,65},{33,97},{65,1},{97,33},{2,66}... | collective-permute-start | bytes 2359304 | tf_op jit(solution)/shard_map/ppermute | solution.py:20
  59.0 63.6 %collective-permute-start.18 = (bf16[256,1536]{1,0:T(8,128)(2,1)}, bf16[256,1536]{1,0:T(8,128)(2,1)}, u32[]{:S(2)}, u32[]{:S(2)}) collective-permute-start(bf16[256,1536]{1,0:T(8,128)(2,1)} %get-tuple-element.12), channel_id=1, source_target_pairs={{0,32},{32,64},{64,96},{96,0},{1,33},{33,65},{65,97},{97,1},{2,34}... | collective-permute-start | bytes 2359304 | tf_op jit(solution)/shard_map/ppermute | solution.py:20
  107.0 34.9 %collective-permute-start.7 = (bf16[256,768]{1,0:T(8,128)(2,1)}, bf16[256,768]{1,0:T(8,128)(2,1)}, u32[]{:S(2)}, u32[]{:S(2)}) collective-permute-start(bf16[256,768]{1,0:T(8,128)(2,1)} %get-tuple-element.13), channel_id=1, source_target_pairs={{0,1},{1,2},{2,3},{3,0},{4,5},{5,6},{6,7},{7,4},{8,9},{9,10},{10,1... | collective-permute-start | bytes 1179656 | tf_op jit(solution)/shard_map/ppermute | solution.py:20
  122.5 13.2 %collective-permute-start.12 = (bf16[256,768]{1,0:T(8,128)(2,1)S(1)}, bf16[256,768]{1,0:T(8,128)(2,1)S(1)}, u32[]{:S(2)}, u32[]{:S(2)}) collective-permute-start(bf16[256,768]{1,0:T(8,128)(2,1)S(1)} %get-tuple-element.14), channel_id=1, source_target_pairs={{0,3},{1,0},{2,1},{3,2},{4,7},{5,4},{6,5},{7,6},{8,11},{9,8},{10,9... | collective-permute-start | bytes 1179656 | tf_op jit(solution)/shard_map/ppermute | solution.py:20
  128.0 15.3 %collective-permute-start.8 = (bf16[256,768]{1,0:T(8,128)(2,1)}, bf16[256,768]{1,0:T(8,128)(2,1)}, u32[]{:S(2)}, u32[]{:S(2)}) collective-permute-start(bf16[256,768]{1,0:T(8,128)(2,1)} %get-tuple-element.17), channel_id=1, source_target_pairs={{0,3},{1,0},{2,1},{3,2},{4,7},{5,4},{6,5},{7,6},{8,11},{9,8},{10,9... | collective-permute-start | bytes 1179656 | tf_op jit(solution)/shard_map/ppermute | solution.py:20
  135.7 30.1 %collective-permute-start.25 = (bf16[384,1536]{1,0:T(8,128)(2,1)}, bf16[384,1536]{1,0:T(8,128)(2,1)}, u32[]{:S(2)}, u32[]{:S(2)}) collective-permute-start(bf16[384,1536]{1,0:T(8,128)(2,1)} %convolution_convert_fusion.1), channel_id=1, source_target_pairs={{0,8},{8,0},{1,9},{9,1},{2,10},{10,2},{3,11},{11,3},{4,12},{12,4},... | collective-permute-start | bytes 3538952 | tf_op jit(solution)/shard_map/ppermute | solution.py:20
  155.0 16.0 %collective-permute-start.15 = (f32[2,256]{1,0:T(2,128)S(1)}, f32[2,256]{1,0:T(2,128)S(1)}, u32[]{:S(2)}, u32[]{:S(2)}) collective-permute-start(f32[2,256]{1,0:T(2,128)S(1)} %pad_maximum_fusion.2), channel_id=1, source_target_pairs={{0,2},{1,3},{2,0},{3,1},{4,6},{5,7},{6,4},{7,5},{8,10},{9,11},{10,... | collective-permute-start | bytes 6152 | tf_op jit(solution)/shard_map/ppermute | solution.py:20
  158.3 13.8 %collective-permute-start.16 = (f32[2,256]{1,0:T(2,128)S(1)}, f32[2,256]{1,0:T(2,128)S(1)}, u32[]{:S(2)}, u32[]{:S(2)}) collective-permute-start(f32[2,256]{1,0:T(2,128)S(1)} %pad_maximum_fusion.2), channel_id=1, source_target_pairs={{0,3},{1,0},{2,1},{3,2},{4,7},{5,4},{6,5},{7,6},{8,11},{9,8},{10,9... | collective-permute-start | bytes 6152 | tf_op jit(solution)/shard_map/ppermute | solution.py:20
  158.3 13.8 %collective-permute-start.14 = (f32[2,256]{1,0:T(2,128)S(1)}, f32[2,256]{1,0:T(2,128)S(1)}, u32[]{:S(2)}, u32[]{:S(2)}) collective-permute-start(f32[2,256]{1,0:T(2,128)S(1)} %pad_maximum_fusion.2), channel_id=1, source_target_pairs={{0,1},{1,2},{2,3},{3,0},{4,5},{5,6},{6,7},{7,4},{8,9},{9,10},{10,1... | collective-permute-start | bytes 6152 | tf_op jit(solution)/shard_map/ppermute | solution.py:20
  165.8 41.4 %collective-permute-start.24 = (bf16[384,1536]{1,0:T(8,128)(2,1)}, bf16[384,1536]{1,0:T(8,128)(2,1)}, u32[]{:S(2)}, u32[]{:S(2)}) collective-permute-start(bf16[384,1536]{1,0:T(8,128)(2,1)} %convolution_convert_fusion.2), channel_id=1, source_target_pairs={{0,8},{8,0},{1,9},{9,1},{2,10},{10,2},{3,11},{11,3},{4,12},{12,4},... | collective-permute-start | bytes 3538952 | tf_op jit(solution)/shard_map/ppermute | solution.py:20
  171.0 36.2 %collective-permute-start.26 = (bf16[384,1536]{1,0:T(8,128)(2,1)}, bf16[384,1536]{1,0:T(8,128)(2,1)}, u32[]{:S(2)}, u32[]{:S(2)}) collective-permute-start(bf16[384,1536]{1,0:T(8,128)(2,1)} %fusion.5), channel_id=1, source_target_pairs={{0,16},{16,0},{1,17},{17,1},{2,18},{18,2},{3,19},{19,3},{4,20},{20... | collective-permute-start | bytes 3538952 | tf_op jit(solution)/shard_map/ppermute | solution.py:20
  172.2 27.4 %collective-permute-start.17 = (f32[2,256]{1,0:T(2,128)S(1)}, f32[2,256]{1,0:T(2,128)}, u32[]{:S(2)}, u32[]{:S(2)}) collective-permute-start(f32[2,256]{1,0:T(2,128)S(1)} %add_add_fusion.1), channel_id=1, source_target_pairs={{0,4},{4,0},{1,5},{5,1},{2,6},{6,2},{3,7},{7,3},{8,12},{12,8},{9,1... | collective-permute-start | bytes 6152 | tf_op jit(solution)/shard_map/ppermute | solution.py:20
  174.0 26.2 %collective-permute-start.28 = (f32[768]{0:T(1024)S(1)}, f32[768]{0:T(1024)S(1)}, u32[]{:S(2)}, u32[]{:S(2)}) collective-permute-start(f32[768]{0:T(1024)S(1)} %add.342), channel_id=1, source_target_pairs={{0,16},{16,0},{1,17},{17,1},{2,18},{18,2},{3,19},{19,3},{4,20},{20... | collective-permute-start | bytes 9224 | tf_op jit(solution)/shard_map/ppermute | solution.py:20
  (17 other events, 206.2 us)

commit v2 on v0

v2 whole, which is shorter than its diff:
```python
import functools
import jax
import jax.numpy as jnp
from jax import lax
from jax.experimental import pallas as pl
from jax.experimental.pallas import tpu as pltpu
from jax.sharding import Mesh, PartitionSpec as P

epsilon = 1e-06
DP = ("x", "zl", "c")
MP = ("zh", "y")
f32 = jnp.float32
bf16 = jnp.bfloat16


def gelu_slope(values):
    normal_cdf = 0.5 * (1.0 + lax.erf(values * 0.7071067811865476))
    normal_pdf = jnp.exp(-0.5 * values * values) * 0.3989422804014327
    return normal_cdf + values * normal_pdf


def shift(value, axis, step, size):
    return lax.ppermute(value, axis, [(i, (i + step) % size) for i in range(size)])


def after(value, *done):
    return lax.optimization_barrier((value, *done))[0]


def in_hbm(value):
    return pltpu.with_memory_space_constraint(value, pltpu.HBM)


def call(kernel, grid, in_specs, out_specs, out_shape, scratch, name, mib, flops, moved):
    step = pl.pallas_call(
        kernel,
        grid_spec=pltpu.PrefetchScalarGridSpec(
            num_scalar_prefetch=1, grid=grid, in_specs=in_specs, out_specs=out_specs, scratch_shapes=scratch
        ),
        out_shape=[pltpu.HBM(s.shape, s.dtype) for s in out_shape],
        compiler_params=pltpu.CompilerParams(vmem_limit_bytes=mib * 2**20),
        cost_estimate=pl.CostEstimate(flops=flops, bytes_accessed=moved, transcendentals=0),
        name=name,
    )
    return lambda ids, *operands: step(ids, *map(in_hbm, operands))
    return lambda ids, *operands: step(ids, *map(in_hbm, operands))


def whole(shape):
    return pl.BlockSpec(shape, lambda i, ids: (0,) * len(shape))


def along(ref, block, width):
    return ref[:, pl.ds(pl.multiple_of(block * width, 128), width)]


def normalise(parts, ids, wanted, gain, strip):
    n, (rows, own) = len(parts), parts[0].shape
    m = len(wanted)

    def kernel(ids_ref, *refs):
        part_refs, (gain_ref, *refs) = refs[:n], refs[n:]
        normed_ref, mean_ref, inv_ref, *out_refs = refs
        total = sum(jnp.sum(r[...].astype(f32), axis=1, keepdims=True) for r in part_refs)
        mean = total * (1.0 / (n * own))
        square = sum(jnp.sum(jnp.square(r[...].astype(f32) - mean), axis=1, keepdims=True) for r in part_refs)
        inv = lax.rsqrt(square * (1.0 / (n * own)) + epsilon)
        mean_ref[...] = jnp.broadcast_to(mean, (strip, 128))
        inv_ref[...] = jnp.broadcast_to(inv, (strip, 128))
        for k in range(n):
            scaled = (part_refs[k][...].astype(f32) - mean) * inv
            normed = (scaled * along(gain_ref, ids_ref[k], own)).astype(bf16)
            normed_ref[:, pl.ds(pl.multiple_of(ids_ref[k] * own, 128), own)] = normed
        for k in range(m):
            out_refs[k][...] = along(normed_ref, ids_ref[n + k], own)

    def strips(width):
        return pl.BlockSpec((strip, width), lambda i, ids: (i, 0))

    return call(
        kernel,
        (rows // strip,),
        [strips(own)] * n + [whole(gain.shape)],
        [strips(n * own)] + [strips(128)] * 2 + [strips(own)] * m,
        [jax.ShapeDtypeStruct((rows, n * own), bf16)]
        + [jax.ShapeDtypeStruct((rows, 128), f32)] * 2
        + [jax.ShapeDtypeStruct((rows, own), bf16)] * m,
        [],
        "normalise",
        10,
        0,
        10 * n * rows * own,
    )(jnp.stack(ids + wanted), *parts, gain)


def project(normed, w_in, hidden, step):
    rows, width = hidden.shape
    strips = [slice(k * step, (k + 1) * step) for k in range(width // step)]

    def kernel(normed_ref, w_ref, hidden_ref, out_ref, w, done):
        copies = [
            pltpu.make_async_copy(w_ref.at[:, strip], w.at[:, strip], done.at[k]) for k, strip in enumerate(strips)
        ]
        for copy in copies:
            copy.start()
        for copy, strip in zip(copies, strips):
            copy.wait()
            pre = jnp.dot(normed_ref[...], w[:, strip], preferred_element_type=f32)
            out_ref[:, strip] = (hidden_ref[:, strip].astype(f32) * gelu_slope(pre)).astype(bf16)

    return pl.pallas_call(
        kernel,
        grid=(1,),
        in_specs=[
            pl.BlockSpec(normed.shape, lambda j: (0, 0)),
            pl.BlockSpec(memory_space=pl.ANY),
            pl.BlockSpec((rows, width), lambda j: (0, 0)),
        ],
        out_specs=pl.BlockSpec((rows, width), lambda j: (0, 0)),
        out_shape=jax.ShapeDtypeStruct((rows, width), bf16),
        scratch_shapes=[pltpu.VMEM(w_in.shape, bf16), pltpu.SemaphoreType.DMA((len(strips),))],
        compiler_params=pltpu.CompilerParams(vmem_limit_bytes=32 * 2**20),
        cost_estimate=pl.CostEstimate(flops=2 * normed.size * width, bytes_accessed=2 * w_in.size, transcendentals=hidden.size),
        name="project",
    )(normed, in_hbm(w_in), hidden)


def spread(pre_grad, ids, w_in, own, ahead):
    n, (rows, depth) = len(ids), pre_grad.shape

    def kernel(ids_ref, grad_ref, w_ref, *refs):
        out_refs, (blocks, done) = refs[:n], refs[n:]
        copies = [
            pltpu.make_async_copy(
                w_ref.at[pl.ds(pl.multiple_of(ids_ref[k] * own, own), own), :],
                blocks.at[k % ahead],
                done.at[k % ahead],
            )
            for k in range(n)
        ]
        for k in range(ahead):
            copies[k].start()
        for k in range(n):
            copies[k].wait()
            out_refs[k][...] = lax.dot_general(
                grad_ref[...], blocks[k % ahead], (((1,), (1,)), ((), ())), preferred_element_type=f32
            ).astype(bf16)
            if k + ahead < n:
                copies[k + ahead].start()

    return call(
        kernel,
        (1,),
        [whole((rows, depth)), pl.BlockSpec(memory_space=pl.ANY)],
        [whole((rows, own))] * n,
        [jax.ShapeDtypeStruct((rows, own), bf16)] * n,
        [pltpu.VMEM((ahead, own, depth), bf16), pltpu.SemaphoreType.DMA((ahead,))],
        "spread",
        20,
        2 * n * rows * own * depth,
        2 * w_in.size,
    )(jnp.stack(ids), pre_grad, w_in)


def outer(same, crossed, grads, half, width, sides, cores, rows):
    tokens = same[0].shape[0]
    cut = tokens // 2
    terms = [
        [(0, 0, 0, tokens), (1, 0, 1, tokens), (2, 0, 2, tokens), (3, 0, 3, cut), (3, cut, 4, cut)],
        [(0, 0, 0, tokens), (1, 0, 1, tokens), (1, tokens, 3, cut), (2, 0, 2, tokens), (2, tokens, 4, cut)],
    ]

    def kernel(ids_ref, *refs):
        same_refs, crossed_refs, grads_refs, (sent_ref, kept_ref) = refs[:4], refs[4:7], refs[7:12], refs[12:]
        i = pl.program_id(0)
        for side, left_refs in enumerate((same_refs, crossed_refs)):

            @pl.when(ids_ref[i] == side)
            def _():
                column = pl.ds(pl.multiple_of(ids_ref[4 + i] * rows, 128), rows)
                total = None
                for k, at, group, size in terms[side]:
                    term = lax.dot_general(
                        left_refs[k][at : at + size, column],
                        grads_refs[group][...],
                        (((0,), (0,)), ((), ())),
                        preferred_element_type=f32,
                    )
                    total = term if total is None else total + term

                @pl.when(i < 2)
                def _():
                    sent_ref[...] = total.astype(bf16)

                @pl.when(i >= 2)
                def _():
                    kept_ref[...] = total

    return call(
        kernel,
        (4,),
        [whole(p.shape) for p in (*same, *crossed)]
        + [pl.BlockSpec((g.shape[0], width), lambda i, ids: (0, half)) for g in grads],
        [
            pl.BlockSpec((rows, width), lambda i, ids: (jnp.minimum(i, 1), 0)),
            pl.BlockSpec((rows, width), lambda i, ids: (jnp.maximum(i - 2, 0), 0)),
        ],
        [jax.ShapeDtypeStruct((2 * rows, width), bf16), jax.ShapeDtypeStruct((2 * rows, width), f32)],
        [],
        "outer",
        16,
        32 * rows * tokens * width,
        32 * tokens * width,
    )(jnp.stack(sides + cores), *same, *crossed, *grads)


def local(inputs, out_grad, attn_grad, hidden_grad, gain, w_in):
    tokens, own = inputs.shape
    hidden = w_in.shape[1]
    x, zl, c = (lax.axis_index(name) for name in DP)
    zh, y = (lax.axis_index(name) for name in MP)
    gain_row = gain[None, :]
    parity = y % 2
    cut = tokens // 2

    def block(dz, dy):
        return (zh ^ dz) * 4 + (y + dy) % 4

    parts = {(0, 0): inputs}
    parts[1, 0] = shift(inputs, "zh", 1, 2)
    parts[0, 2] = shift(inputs, "y", 2, 4)
    parts[0, 3] = shift(inputs, "y", 1, 4)
    parts[0, 1] = shift(inputs, "y", 3, 4)
    parts[1, 2] = shift(parts[0, 2], "zh", 1, 2)
    parts[1, 3] = shift(parts[1, 0], "y", 1, 4)
    parts[1, 1] = shift(parts[1, 0], "y", 3, 4)
    keys = list(parts)
    wanted = [2 * ((x + step) % 4) + parity for step in range(4)] + [2 * x + 1 - parity]
    normed, mean, inv, *sends, crossed_own = normalise(
        [parts[k] for k in keys], [block(*k) for k in keys], wanted, gain_row, 64
    )

    same = [sends[0], shift(sends[1], "x", 1, 4), shift(sends[3], "x", 3, 4), shift(sends[2], "x", 2, 4)]

    pre_grad = project(normed, w_in, hidden_grad, 512)

    low, high = shift(pre_grad, "x", 1, 4), shift(pre_grad, "x", 3, 4)

    same[3] = after(same[3], pre_grad)
    down = shift(jnp.concatenate([same[1], same[3][:cut]], 0), "y", 3, 4)
    up = shift(jnp.concatenate([same[2], same[3][cut:]], 0), "y", 1, 4)
    crossed = [crossed_own, down, up]

    pieces = dict(zip(keys, spread(pre_grad, [block(*k) for k in keys], w_in, own, 4)))
    got_z = shift(pieces[1, 2], "zh", 1, 2)
    got_p = shift(after(pieces[1, 1], down, up), "y", 1, 4)
    got_m = shift(after(pieces[1, 3], down, up), "y", 3, 4)
    near_p = shift(after(pieces[0, 1], got_p, got_m), "y", 1, 4)
    near_m = shift(after(pieces[0, 3], got_p, got_m), "y", 3, 4)
    far = shift((pieces[0, 2].astype(f32) + got_z.astype(f32)).astype(bf16), "y", 2, 4)
    across = shift((pieces[1, 0].astype(f32) + got_p.astype(f32) + got_m.astype(f32)).astype(bf16), "zh", 1, 2)

    far_low = shift(after(low[:cut], pieces[0, 0]), "x", 1, 4)
    far_high = shift(after(high[cut:], pieces[0, 0]), "x", 3, 4)
    grads = [pre_grad, low, high, far_low, far_high]

    rows = own // 2
    sides = [zl ^ 1 ^ parity, zl ^ parity] * 2
    cores = [1 - c, 1 - c, c, c]
    weight_parts = []
    got = None
    for half in (0, 1):
        sent, kept = outer(same, crossed, grads, half, hidden // 2, sides, cores, rows)
        got_c = shift(sent, "c", 1, 2)
        if got is not None:
            got_c = after(got_c, got)
        got = shift((kept[:rows] + got_c[:rows].astype(f32)).astype(bf16), "zl", 1, 2)
        weight_parts.append((kept[rows:] + got_c[rows:].astype(f32)) + got.astype(f32))
    weight_grad = jnp.concatenate(weight_parts, 1)

    mean, inv = mean[:, :1], inv[:, :1]
    scaled_own = (inputs.astype(f32) - mean) * inv
    gain_own = lax.dynamic_slice_in_dim(gain, block(0, 0) * own, own, 0)
    dnorm = attn_grad.astype(f32) + pieces[0, 0].astype(f32)
    for value in (near_p, near_m, far, across):
        dnorm = dnorm + value.astype(f32)
    dxhat = dnorm * gain_own
    sums = jnp.stack([jnp.sum(dxhat, axis=1), jnp.sum(dxhat * scaled_own, axis=1)])
    for axis, step, size in (("zh", 1, 2), ("y", 2, 4), ("y", 1, 4)):
        sums = sums + shift(sums, axis, step, size)
    sums = sums * (1.0 / (own * 8))
    first_mean, second_mean = sums[0][:, None], sums[1][:, None]
    input_grad = (out_grad.astype(f32) + inv * (dxhat - first_mean - scaled_own * second_mean)).astype(bf16)
    gain_grad = jnp.sum(dnorm * scaled_own, axis=0)
    for axis, step, size in (("c", 1, 2), ("zl", 1, 2), ("x", 2, 4), ("x", 1, 4)):
        gain_grad = gain_grad + shift(gain_grad, axis, step, size)
    return (input_grad, weight_grad, gain_grad)


def solution(mesh):
    fine = Mesh(mesh.devices.reshape(4, 2, 2, 2, 4), DP + MP)
    both = P(DP, MP)
    in_specs = (both, both, both, both, P(), P(None, MP))
    out_specs = (both, both, P(MP))
    return jax.shard_map(local, mesh=fine, in_specs=in_specs, out_specs=out_specs, check_vma=False)
```

time: 453 us -> 160 us (0.35); the launches traced: 446 us -> 159 us
  waiting for transfers between devices: 352 us -> 62.3 us
  Pallas kernels: 0 us -> 44.9 us
  starting transfers between devices: 0.16 us -> 40.1 us
  blocking collectives: 34.2 us -> 0 us
  matrix products: 31.6 us -> 0 us
  between operations: 13.8 us -> 0.98 us
  other arithmetic: 13.3 us -> 5.13 us
    reduce_scatter x1 -> x0, waiting for transfers between devices: 159 us -> none  [local(): lax.psum_scatter(lax.dot_general(normed, pre_grad, (((0,), (0,)), ((), ()...]
    psum x1 -> x0, waiting for transfers between devices: 99 us -> none  [local(): summed = lax.psum(input_term.astype(jnp.bfloat16), 'mp').astype(jnp.float32)]
    all_gather x2 -> x0, waiting for transfers between devices: 92 us -> none  [the longest x1 65.6 us: local(): gathered = lax.all_gather(inputs, 'mp', axis=1, tiled=True)]
    ppermute x0 -> x34, waiting for transfers between devices: none -> 62.3 us  [shift(): lax.ppermute(value, axis, [(i, (i + step) % size) for i in range(size)])]
    pallas_call x0 -> x5, Pallas kernels: none -> 44.9 us  [the longest x4 36.2 us: call(): return lambda ids, *operands: step(ids, *map(in_hbm, operands))]
    ppermute x0 -> x34, starting transfers between devices: none -> 40.1 us  [shift(): lax.ppermute(value, axis, [(i, (i + step) % size) for i in range(size)])]
    psum x1 -> x0, blocking collectives: 34.2 us -> none  [local(): gain_grad = lax.psum(jnp.sum(dnorm_own * scaled_own, axis=0), 'dp')]
    dot_general x3 -> x0, matrix products: 31.6 us -> none  [the longest x1 11.5 us: local(): lax.dot_general(normed, pre_grad, (((0,), (0,)), ((), ())), preferred_ele...]
  transfers between devices with their start and end apart: 4 -> 34, of which waited for: 4 -> 18; matrix products, arithmetic and copies ran while one was open for 9% -> 3% of each run, Pallas kernels for 0% -> 24%
where the time goes in v2:
time: 160 us; the launch traced here: 159 us
  waiting for transfers between devices  62.3 us (39%)
  Pallas kernels  44.9 us (28%)
  starting transfers between devices  40.1 us (25%)
  other arithmetic  5.13 us (3%)
  local copies, waits for them, and re-layouts  5.05 us (3%)
    ppermute x34, waiting for transfers between devices, shift(): lax.ppermute(value, axis, [(i, (i + step) % size) for i in range(size)])  62.3 us
    ppermute x34, starting transfers between devices, shift(): lax.ppermute(value, axis, [(i, (i + step) % size) for i in range(size)])  40.1 us
    pallas_call x4, Pallas kernels, call(): return lambda ids, *operands: step(ids, *map(in_hbm, operands))  36.2 us
    pallas_call x1, Pallas kernels, project(): pl.pallas_call(kernel, grid=(1,), in_specs=[pl.BlockSpec(normed.shape, la...  8.67 us
    unnamed x60, local copies, waits for them, and re-layouts  3.74 us
  transfers between devices with their start and end apart: 34, of which 18 were waited for; matrix products, arithmetic and copies ran while one was open for 3% of the time, Pallas kernels for 24%

profile of v2, /device:TPU:24, one launch (start us, length us, event | category | flops | bytes accessed | tf_op | source)
XLA Modules:
  0.0 158.6 jit_solution(1322484763466956333)
XLA Ops:
  0.6 4.0 %collective-permute-start = (bf16[256,768]{1,0:T(8,128)(2,1)}, bf16[256,768]{1,0:T(8,128)(2,1)S(1)}, u32[]{:S(2)}, u32[]{:S(2)}) collective-permute-start(bf16[256,768]{1,0:T(8,128)(2,1)} %refs_0_.1), channel_id=1, source_target_pairs={{0,4},{4,0},{1,5},{5,1},{2,6},{6,2},{3,7},{7,3},{8,12},{12,8},{9,1... | collective-permute-start | bytes 1179656 | tf_op jit(solution)/shard_map/ppermute | solution.py:23
  5.8 2.2 %collective-permute-start.2 = (bf16[256,768]{1,0:T(8,128)(2,1)}, bf16[256,768]{1,0:T(8,128)(2,1)S(1)}, u32[]{:S(2)}, u32[]{:S(2)}) collective-permute-start(bf16[256,768]{1,0:T(8,128)(2,1)} %refs_0_.1), channel_id=1, source_target_pairs={{0,1},{1,2},{2,3},{3,0},{4,5},{5,6},{6,7},{7,4},{8,9},{9,10},{10,1... | collective-permute-start | bytes 1179656 | tf_op jit(solution)/shard_map/ppermute | solution.py:23
  8.0 5.9 %collective-permute-done.refs_1_ = bf16[256,768]{1,0:T(8,128)(2,1)S(1)} collective-permute-done((bf16[256,768]{1,0:T(8,128)(2,1)}, bf16[256,768]{1,0:T(8,128)(2,1)S(1)}, u32[]{:S(2)}, u32[]{:S(2)}) %collective-permute-start) | collective-permute-done | bytes 393248 | tf_op jit(solution)/shard_map/ppermute | solution.py:23
  15.9 2.4 %collective-permute-done.1.refs_2_ = bf16[256,768]{1,0:T(8,128)(2,1)S(1)} collective-permute-done((bf16[256,768]{1,0:T(8,128)(2,1)}, bf16[256,768]{1,0:T(8,128)(2,1)S(1)}, u32[]{:S(2)}, u32[]{:S(2)}) %collective-permute-start.1) | collective-permute-done | bytes 393248 | tf_op jit(solution)/shard_map/ppermute | solution.py:23
  19.4 5.0 %collective-permute-done.2.refs_3_ = bf16[256,768]{1,0:T(8,128)(2,1)S(1)} collective-permute-done((bf16[256,768]{1,0:T(8,128)(2,1)}, bf16[256,768]{1,0:T(8,128)(2,1)S(1)}, u32[]{:S(2)}, u32[]{:S(2)}) %collective-permute-start.2) | collective-permute-done | bytes 393248 | tf_op jit(solution)/shard_map/ppermute | solution.py:23
  25.4 5.9 %collective-permute-done.5.refs_6_ = bf16[256,768]{1,0:T(8,128)(2,1)S(1)} collective-permute-done((bf16[256,768]{1,0:T(8,128)(2,1)S(1)}, bf16[256,768]{1,0:T(8,128)(2,1)S(1)}, u32[]{:S(2)}, u32[]{:S(2)}) %collective-permute-start.5) | collective-permute-done | bytes 393248 | tf_op jit(solution)/shard_map/ppermute | solution.py:23
  31.3 2.4 %collective-permute-done.6.refs_7_ = bf16[256,768]{1,0:T(8,128)(2,1)S(1)} collective-permute-done((bf16[256,768]{1,0:T(8,128)(2,1)S(1)}, bf16[256,768]{1,0:T(8,128)(2,1)S(1)}, u32[]{:S(2)}, u32[]{:S(2)}) %collective-permute-start.6) | collective-permute-done | bytes 393248 | tf_op jit(solution)/shard_map/ppermute | solution.py:23
  34.6 6.9 %normalise.1 = (bf16[256,6144]{1,0:T(8,128)(2,1)}, f32[256,128]{1,0:T(8,128)}, f32[256,128]{1,0:T(8,128)}, bf16[256,768]{1,0:T(8,128)(2,1)}, bf16[256,768]{1,0:T...) custom-call(s32[13]{0:T(128)S(1)} %stack.103.ids_ref, ...), custom_call_target="tpu_custom_call" | custom-call | bytes 15728640 | tf_op jit(solution)/shard_map/normalise/pallas_call | solution.py:45
  41.5 3.1 %collective-permute-start.8 = (bf16[256,768]{1,0:T(8,128)(2,1)}, bf16[256,768]{1,0:T(8,128)(2,1)S(1)}, u32[]{:S(2)}, u32[]{:S(2)}) collective-permute-start(bf16[256,768]{1,0:T(8,128)(2,1)} %get-tuple-element.37), channel_id=1, source_target_pairs={{0,64},{32,96},{64,0},{96,32},{1,65},{33,97},{65,1},{97,33},{2,66}... | collective-permute-start | bytes 1179656 | tf_op jit(solution)/shard_map/ppermute | solution.py:23
  46.6 1.9 %copy-done.1 = bf16[256,6144]{1,0:T(8,128)(2,1)S(1)} copy-done((bf16[256,6144]{1,0:T(8,128)(2,1)S(1)}, bf16[256,6144]{1,0:T(8,128)(2,1)}, u32[]{:S(2)}) %copy-start.1) | copy-done | bytes 3145752
  48.5 8.7 %project.1.grad_ref.refs_7_ = bf16[256,1536]{1,0:T(8,128)(2,1)S(1)} custom-call(bf16[256,6144]{1,0:T(8,128)(2,1)S(1)} %copy-done.1, bf16[6144,1536]{1,0:T(8,128)(2,1)} %w_ref.3, bf16[256,1536]{1,0:T(8,128)(2,1)S(1)} %copy-done.2), custom_call_target="tpu_custom_call" | custom-call | flops 4831838208 | bytes 18874368 | tf_op jit(solution)/shard_map/project/pallas_call | solution.py:111
  57.9 2.6 %collective-permute-start.23 = (bf16[256,1536]{1,0:T(8,128)(2,1)S(1)}, bf16[256,1536]{1,0:T(8,128)(2,1)S(1)}, u32[]{:S(2)}, u32[]{:S(2)}) collective-permute-start(bf16[256,1536]{1,0:T(8,128)(2,1)S(1)} %project.1.grad_ref.refs_7_), channel_id=1, source_target_pairs={{0,96},{32,0},{64,32},{96,64},{1,97},{33,1},{65,33},{97,65},{2,98}... | collective-permute-start | bytes 2359304 | tf_op jit(solution)/shard_map/ppermute | solution.py:23
  60.6 3.3 %collective-permute-done.10.refs_2_ = bf16[256,768]{1,0:T(8,128)(2,1)S(1)} collective-permute-done((bf16[256,768]{1,0:T(8,128)(2,1)}, bf16[256,768]{1,0:T(8,128)(2,1)S(1)}, u32[]{:S(2)}, u32[]{:S(2)}) %collective-permute-start.10) | collective-permute-done | bytes 393248 | tf_op jit(solution)/shard_map/ppermute | solution.py:23
  66.3 12.2 %spread.1 = (bf16[256,768]{1,0:T(8,128)(2,1)}, bf16[256,768]{1,0:T(8,128)(2,1)}, bf16[256,768]{1,0:T(8,128)(2,1)}, bf16[256,768]{1,0:T(8,128)(2,1)}, bf16[256,76...) custom-call(s32[8]{0:T(128)S(1)} %stack.104.ids_ref, ...), custom_call_target="tpu_custom_call" | custom-call | flops 4831838208 | bytes 18874368 | tf_op jit(solution)/shard_map/spread/pallas_call | solution.py:45
  86.4 5.7 %collective-permute-done.24.refs_10_ = bf16[128,1536]{1,0:T(8,128)(2,1)S(1)} collective-permute-done((bf16[128,1536]{1,0:T(8,128)(2,1)S(1)}, bf16[128,1536]{1,0:T(8,128)(2,1)S(1)}, u32[]{:S(2)}, u32[]{:S(2)}) %collective-permute-start.24) | collective-permute-done | bytes 393248 | tf_op jit(solution)/shard_map/ppermute | solution.py:23
  93.0 8.6 %outer.2 = (bf16[768,768]{1,0:T(8,128)(2,1)}, f32[768,768]{1,0:T(8,128)}) custom-call(s32[8]{0:T(128)S(1)} %stack.112.ids_ref, bf16[256,768]{1,0:T(8,128)(2,1)} %get-tuple-element.50.refs_0_, bf16[256,768]{1,0:T(8,128)(2,1)} %copy-done.8, bf16[256,768]{1,0:T(8,128)(2,1)} %copy-done.7, bf16[256,768]{1,0:T(8,128)(2,1)} %copy-done.6, ...), custom_call_target="tpu_custom_call" | custom-call | flops 2415919104 | bytes 6291456 | tf_op jit(solution)/shard_map/outer/pallas_call | solution.py:45
  106.2 8.6 %outer.3 = (bf16[768,768]{1,0:T(8,128)(2,1)}, f32[768,768]{1,0:T(8,128)}) custom-call(s32[8]{0:T(128)S(1)} %stack.112.ids_ref, bf16[256,768]{1,0:T(8,128)(2,1)} %get-tuple-element.50.refs_0_, bf16[256,768]{1,0:T(8,128)(2,1)} %copy-done.8, bf16[256,768]{1,0:T(8,128)(2,1)} %copy-done.7, bf16[256,768]{1,0:T(8,128)(2,1)} %copy-done.6, ...), custom_call_target="tpu_custom_call" | custom-call | flops 2415919104 | bytes 6291456 | tf_op jit(solution)/shard_map/outer/pallas_call | solution.py:45
  115.3 5.6 %collective-permute-done.14 = bf16[256,768]{1,0:T(8,128)(2,1)S(1)} collective-permute-done((bf16[256,768]{1,0:T(8,128)(2,1)S(1)}, bf16[256,768]{1,0:T(8,128)(2,1)S(1)}, u32[]{:S(2)}, u32[]{:S(2)}) %collective-permute-start.14) | collective-permute-done | bytes 393248 | tf_op jit(solution)/shard_map/ppermute | solution.py:23
  120.9 2.4 %collective-permute-done.15 = bf16[256,768]{1,0:T(8,128)(2,1)S(1)} collective-permute-done((bf16[256,768]{1,0:T(8,128)(2,1)S(1)}, bf16[256,768]{1,0:T(8,128)(2,1)S(1)}, u32[]{:S(2)}, u32[]{:S(2)}) %collective-permute-start.15) | collective-permute-done | bytes 393248 | tf_op jit(solution)/shard_map/ppermute | solution.py:23
  125.9 3.3 %collective-permute-done.19 = f32[2,256]{1,0:T(2,128)S(1)} collective-permute-done((f32[2,256]{1,0:T(2,128)S(1)}, f32[2,256]{1,0:T(2,128)S(1)}, u32[]{:S(2)}, u32[]{:S(2)}) %collective-permute-start.19) | collective-permute-done | bytes 2080 | tf_op jit(solution)/shard_map/ppermute | solution.py:23
  131.5 2.9 %collective-permute-done.20 = f32[2,256]{1,0:T(2,128)S(1)} collective-permute-done((f32[2,256]{1,0:T(2,128)S(1)}, f32[2,256]{1,0:T(2,128)S(1)}, u32[]{:S(2)}, u32[]{:S(2)}) %collective-permute-start.20) | collective-permute-done | bytes 2080 | tf_op jit(solution)/shard_map/ppermute | solution.py:23
  135.1 5.1 %collective-permute-done.31 = f32[768]{0:T(1024)S(1)} collective-permute-done((f32[768]{0:T(1024)S(1)}, f32[768]{0:T(1024)S(1)}, u32[]{:S(2)}, u32[]{:S(2)}) %collective-permute-start.31) | collective-permute-done | bytes 3104 | tf_op jit(solution)/shard_map/ppermute | solution.py:23
  147.9 2.3 %collective-permute-done.33 = f32[768]{0:T(1024)S(1)} collective-permute-done((f32[768]{0:T(1024)S(1)}, f32[768]{0:T(1024)S(1)}, u32[]{:S(2)}, u32[]{:S(2)}) %collective-permute-start.33) | collective-permute-done | bytes 3104 | tf_op jit(solution)/shard_map/ppermute | solution.py:23
  151.0 5.7 %collective-permute-done.29 = bf16[384,768]{1,0:T(8,128)(2,1)S(1)} collective-permute-done((bf16[384,768]{1,0:T(8,128)(2,1)S(1)}, bf16[384,768]{1,0:T(8,128)(2,1)S(1)}, u32[]{:S(2)}, u32[]{:S(2)}) %collective-permute-start.29) | collective-permute-done | bytes 589856 | tf_op jit(solution)/shard_map/ppermute | solution.py:23
  (138 shorter events, 41.1 us)
Async XLA Ops:
  4.6 13.8 %collective-permute-start.1 = (bf16[256,768]{1,0:T(8,128)(2,1)}, bf16[256,768]{1,0:T(8,128)(2,1)S(1)}, u32[]{:S(2)}, u32[]{:S(2)}) collective-permute-start(bf16[256,768]{1,0:T(8,128)(2,1)} %refs_0_.1), channel_id=1, source_target_pairs={{0,2},{1,3},{2,0},{3,1},{4,6},{5,7},{6,4},{7,5},{8,10},{9,11},{10,... | collective-permute-start | bytes 1179656 | tf_op jit(solution)/shard_map/ppermute | solution.py:23
  5.8 18.5 %collective-permute-start.2 = (bf16[256,768]{1,0:T(8,128)(2,1)}, bf16[256,768]{1,0:T(8,128)(2,1)S(1)}, u32[]{:S(2)}, u32[]{:S(2)}) collective-permute-start(bf16[256,768]{1,0:T(8,128)(2,1)} %refs_0_.1), channel_id=1, source_target_pairs={{0,1},{1,2},{2,3},{3,0},{4,5},{5,6},{6,7},{7,4},{8,9},{9,10},{10,1... | collective-permute-start | bytes 1179656 | tf_op jit(solution)/shard_map/ppermute | solution.py:23
  8.0 17.4 %collective-permute-start.3 = (bf16[256,768]{1,0:T(8,128)(2,1)}, bf16[256,768]{1,0:T(8,128)(2,1)S(1)}, u32[]{:S(2)}, u32[]{:S(2)}) collective-permute-start(bf16[256,768]{1,0:T(8,128)(2,1)} %refs_0_.1), channel_id=1, source_target_pairs={{0,3},{1,0},{2,1},{3,2},{4,7},{5,4},{6,5},{7,6},{8,11},{9,8},{10,9... | collective-permute-start | bytes 1179656 | tf_op jit(solution)/shard_map/ppermute | solution.py:23
  13.9 17.4 %collective-permute-start.5 = (bf16[256,768]{1,0:T(8,128)(2,1)S(1)}, bf16[256,768]{1,0:T(8,128)(2,1)S(1)}, u32[]{:S(2)}, u32[]{:S(2)}) collective-permute-start(bf16[256,768]{1,0:T(8,128)(2,1)S(1)} %collective-permute-done.refs_1_), channel_id=1, source_target_pairs={{0,1},{1,2},{2,3},{3,0},{4,5},{5,6},{6,7},{7,4},{8,9},{9,10},{10,1... | collective-permute-start | bytes 1179656 | tf_op jit(solution)/shard_map/ppermute | solution.py:23
  14.1 19.6 %collective-permute-start.6 = (bf16[256,768]{1,0:T(8,128)(2,1)S(1)}, bf16[256,768]{1,0:T(8,128)(2,1)S(1)}, u32[]{:S(2)}, u32[]{:S(2)}) collective-permute-start(bf16[256,768]{1,0:T(8,128)(2,1)S(1)} %collective-permute-done.refs_1_), channel_id=1, source_target_pairs={{0,3},{1,0},{2,1},{3,2},{4,7},{5,4},{6,5},{7,6},{8,11},{9,8},{10,9... | collective-permute-start | bytes 1179656 | tf_op jit(solution)/shard_map/ppermute | solution.py:23
  18.4 15.3 %collective-permute-start.4 = (bf16[256,768]{1,0:T(8,128)(2,1)S(1)}, bf16[256,768]{1,0:T(8,128)(2,1)S(1)}, u32[]{:S(2)}, u32[]{:S(2)}) collective-permute-start(bf16[256,768]{1,0:T(8,128)(2,1)S(1)} %collective-permute-done.1.refs_2_), channel_id=1, source_target_pairs={{0,4},{4,0},{1,5},{5,1},{2,6},{6,2},{3,7},{7,3},{8,12},{12,8},{9,1... | collective-permute-start | bytes 1179656 | tf_op jit(solution)/shard_map/ppermute | solution.py:23
  41.5 19.0 %collective-permute-start.8 = (bf16[256,768]{1,0:T(8,128)(2,1)}, bf16[256,768]{1,0:T(8,128)(2,1)S(1)}, u32[]{:S(2)}, u32[]{:S(2)}) collective-permute-start(bf16[256,768]{1,0:T(8,128)(2,1)} %get-tuple-element.37), channel_id=1, source_target_pairs={{0,64},{32,96},{64,0},{96,32},{1,65},{33,97},{65,1},{97,33},{2,66}... | collective-permute-start | bytes 1179656 | tf_op jit(solution)/shard_map/ppermute | solution.py:23
  44.6 19.2 %collective-permute-start.10 = (bf16[256,768]{1,0:T(8,128)(2,1)}, bf16[256,768]{1,0:T(8,128)(2,1)S(1)}, u32[]{:S(2)}, u32[]{:S(2)}) collective-permute-start(bf16[256,768]{1,0:T(8,128)(2,1)} %get-tuple-element.39), channel_id=1, source_target_pairs={{0,96},{32,0},{64,32},{96,64},{1,97},{33,1},{65,33},{97,65},{2,98}... | collective-permute-start | bytes 1179656 | tf_op jit(solution)/shard_map/ppermute | solution.py:23
  45.8 18.8 %collective-permute-start.7 = (bf16[256,768]{1,0:T(8,128)(2,1)}, bf16[256,768]{1,0:T(8,128)(2,1)S(1)}, u32[]{:S(2)}, u32[]{:S(2)}) collective-permute-start(bf16[256,768]{1,0:T(8,128)(2,1)} %get-tuple-element.36), channel_id=1, source_target_pairs={{0,32},{32,64},{64,96},{96,0},{1,33},{33,65},{65,97},{97,1},{2,34}... | collective-permute-start | bytes 1179656 | tf_op jit(solution)/shard_map/ppermute | solution.py:23
  57.2 22.4 %collective-permute-start.22 = (bf16[256,1536]{1,0:T(8,128)(2,1)S(1)}, bf16[256,1536]{1,0:T(8,128)(2,1)S(1)}, u32[]{:S(2)}, u32[]{:S(2)}) collective-permute-start(bf16[256,1536]{1,0:T(8,128)(2,1)S(1)} %project.1.grad_ref.refs_7_), channel_id=1, source_target_pairs={{0,32},{32,64},{64,96},{96,0},{1,33},{33,65},{65,97},{97,1},{2,34}... | collective-permute-start | bytes 2359304 | tf_op jit(solution)/shard_map/ppermute | solution.py:23
  57.9 23.4 %collective-permute-start.23 = (bf16[256,1536]{1,0:T(8,128)(2,1)S(1)}, bf16[256,1536]{1,0:T(8,128)(2,1)S(1)}, u32[]{:S(2)}, u32[]{:S(2)}) collective-permute-start(bf16[256,1536]{1,0:T(8,128)(2,1)S(1)} %project.1.grad_ref.refs_7_), channel_id=1, source_target_pairs={{0,96},{32,0},{64,32},{96,64},{1,97},{33,1},{65,33},{97,65},{2,98}... | collective-permute-start | bytes 2359304 | tf_op jit(solution)/shard_map/ppermute | solution.py:23
  63.9 20.4 %collective-permute-start.11 = (bf16[384,768]{1,0:T(8,128)(2,1)S(1)}, bf16[384,768]{1,0:T(8,128)(2,1)}, u32[]{:S(2)}, u32[]{:S(2)}) collective-permute-start(bf16[384,768]{1,0:T(8,128)(2,1)S(1)} %pad_maximum_fusion.2), channel_id=1, source_target_pairs={{0,1},{1,2},{2,3},{3,0},{4,5},{5,6},{6,7},{7,4},{8,9},{9,10},{10,1... | collective-permute-start | bytes 1769480 | tf_op jit(solution)/shard_map/ppermute | solution.py:23
  64.7 19.6 %collective-permute-start.9 = (bf16[384,768]{1,0:T(8,128)(2,1)S(1)}, bf16[384,768]{1,0:T(8,128)(2,1)}, u32[]{:S(2)}, u32[]{:S(2)}) collective-permute-start(bf16[384,768]{1,0:T(8,128)(2,1)S(1)} %pad_maximum_fusion.1), channel_id=1, source_target_pairs={{0,3},{1,0},{2,1},{3,2},{4,7},{5,4},{6,5},{7,6},{8,11},{9,8},{10,9... | collective-permute-start | bytes 1769480 | tf_op jit(solution)/shard_map/ppermute | solution.py:23
  83.1 18.6 %collective-permute-start.16 = (bf16[256,768]{1,0:T(8,128)(2,1)}, bf16[256,768]{1,0:T(8,128)(2,1)S(1)}, u32[]{:S(2)}, u32[]{:S(2)}) collective-permute-start(bf16[256,768]{1,0:T(8,128)(2,1)} %get-tuple-element.47), channel_id=1, source_target_pairs={{0,4},{4,0},{1,5},{5,1},{2,6},{6,2},{3,7},{7,3},{8,12},{12,8},{9,1... | collective-permute-start | bytes 1179656 | tf_op jit(solution)/shard_map/ppermute | solution.py:23
  84.3 18.7 %collective-permute-start.12 = (bf16[256,768]{1,0:T(8,128)(2,1)}, bf16[256,768]{1,0:T(8,128)(2,1)S(1)}, u32[]{:S(2)}, u32[]{:S(2)}) collective-permute-start(bf16[256,768]{1,0:T(8,128)(2,1)} %get-tuple-element.40), channel_id=1, source_target_pairs={{0,1},{1,2},{2,3},{3,0},{4,5},{5,6},{6,7},{7,4},{8,9},{9,10},{10,1... | collective-permute-start | bytes 1179656 | tf_op jit(solution)/shard_map/ppermute | solution.py:23
  85.2 17.8 %collective-permute-start.13 = (bf16[256,768]{1,0:T(8,128)(2,1)S(1)}, bf16[256,768]{1,0:T(8,128)(2,1)S(1)}, u32[]{:S(2)}, u32[]{:S(2)}) collective-permute-start(bf16[256,768]{1,0:T(8,128)(2,1)S(1)} %copy-done.29), channel_id=1, source_target_pairs={{0,3},{1,0},{2,1},{3,2},{4,7},{5,4},{6,5},{7,6},{8,11},{9,8},{10,9... | collective-permute-start | bytes 1179656 | tf_op jit(solution)/shard_map/ppermute | solution.py:23
  101.6 23.0 %collective-permute-start.26 = (bf16[768,768]{1,0:T(8,128)(2,1)}, bf16[768,768]{1,0:T(8,128)(2,1)S(1)}, u32[]{:S(2)}, u32[]{:S(2)}) collective-permute-start(bf16[768,768]{1,0:T(8,128)(2,1)} %get-tuple-element.55), channel_id=1, source_target_pairs={{0,8},{8,0},{1,9},{9,1},{2,10},{10,2},{3,11},{11,3},{4,12},{12,4},... | collective-permute-start | bytes 3538952 | tf_op jit(solution)/shard_map/ppermute | solution.py:23
  101.8 13.5 %collective-permute-start.17 = (bf16[256,768]{1,0:T(8,128)(2,1)S(1)}, bf16[256,768]{1,0:T(8,128)(2,1)S(1)}, u32[]{:S(2)}, u32[]{:S(2)}) collective-permute-start(bf16[256,768]{1,0:T(8,128)(2,1)S(1)} %add_convert_fusion.4), channel_id=1, source_target_pairs={{0,2},{1,3},{2,0},{3,1},{4,6},{5,7},{6,4},{7,5},{8,10},{9,11},{10,... | collective-permute-start | bytes 1179656 | tf_op jit(solution)/shard_map/ppermute | solution.py:23
  103.0 17.9 %collective-permute-start.14 = (bf16[256,768]{1,0:T(8,128)(2,1)S(1)}, bf16[256,768]{1,0:T(8,128)(2,1)S(1)}, u32[]{:S(2)}, u32[]{:S(2)}) collective-permute-start(bf16[256,768]{1,0:T(8,128)(2,1)S(1)} %copy-done.26), channel_id=1, source_target_pairs={{0,1},{1,2},{2,3},{3,0},{4,5},{5,6},{6,7},{7,4},{8,9},{9,10},{10,1... | collective-permute-start | bytes 1179656 | tf_op jit(solution)/shard_map/ppermute | solution.py:23
  103.8 19.5 %collective-permute-start.15 = (bf16[256,768]{1,0:T(8,128)(2,1)S(1)}, bf16[256,768]{1,0:T(8,128)(2,1)S(1)}, u32[]{:S(2)}, u32[]{:S(2)}) collective-permute-start(bf16[256,768]{1,0:T(8,128)(2,1)S(1)} %copy-done.25), channel_id=1, source_target_pairs={{0,3},{1,0},{2,1},{3,2},{4,7},{5,4},{6,5},{7,6},{8,11},{9,8},{10,9... | collective-permute-start | bytes 1179656 | tf_op jit(solution)/shard_map/ppermute | solution.py:23
  105.3 18.0 %collective-permute-start.18 = (bf16[256,768]{1,0:T(8,128)(2,1)S(1)}, bf16[256,768]{1,0:T(8,128)(2,1)S(1)}, u32[]{:S(2)}, u32[]{:S(2)}) collective-permute-start(bf16[256,768]{1,0:T(8,128)(2,1)S(1)} %add_convert_fusion.3), channel_id=1, source_target_pairs={{0,4},{4,0},{1,5},{5,1},{2,6},{6,2},{3,7},{7,3},{8,12},{12,8},{9,1... | collective-permute-start | bytes 1179656 | tf_op jit(solution)/shard_map/ppermute | solution.py:23
  115.3 26.7 %collective-permute-start.28 = (bf16[768,768]{1,0:T(8,128)(2,1)}, bf16[768,768]{1,0:T(8,128)(2,1)S(1)}, u32[]{:S(2)}, u32[]{:S(2)}) collective-permute-start(bf16[768,768]{1,0:T(8,128)(2,1)} %get-tuple-element.57), channel_id=1, source_target_pairs={{0,8},{8,0},{1,9},{9,1},{2,10},{10,2},{3,11},{11,3},{4,12},{12,4},... | collective-permute-start | bytes 3538952 | tf_op jit(solution)/shard_map/ppermute | solution.py:23
  124.7 17.4 %collective-permute-start.27 = (bf16[384,768]{1,0:T(8,128)(2,1)S(1)}, bf16[384,768]{1,0:T(8,128)(2,1)S(1)}, u32[]{:S(2)}, u32[]{:S(2)}) collective-permute-start(bf16[384,768]{1,0:T(8,128)(2,1)S(1)} %add_convert_fusion.1), channel_id=1, source_target_pairs={{0,16},{16,0},{1,17},{17,1},{2,18},{18,2},{3,19},{19,3},{4,20},{20... | collective-permute-start | bytes 1769480 | tf_op jit(solution)/shard_map/ppermute | solution.py:23
  142.3 14.4 %collective-permute-start.29 = (bf16[384,768]{1,0:T(8,128)(2,1)S(1)}, bf16[384,768]{1,0:T(8,128)(2,1)S(1)}, u32[]{:S(2)}, u32[]{:S(2)}) collective-permute-start(bf16[384,768]{1,0:T(8,128)(2,1)S(1)} %add_convert_fusion), channel_id=1, source_target_pairs={{0,16},{16,0},{1,17},{17,1},{2,18},{18,2},{3,19},{19,3},{4,20},{20... | collective-permute-start | bytes 1769480 | tf_op jit(solution)/shard_map/ppermute | solution.py:23
  (40 other events, 298.8 us)

commit v3 on v2

--- a/solution.py
+++ b/solution.py
@@ -31,13 +31,13 @@
     return pltpu.with_memory_space_constraint(value, pltpu.HBM)
 
 
-def call(kernel, grid, in_specs, out_specs, out_shape, scratch, name, mib, flops, moved):
+def call(kernel, grid, in_specs, out_specs, out_shape, scratch, name, mib, flops, moved, free=0):
     step = pl.pallas_call(
         kernel,
         grid_spec=pltpu.PrefetchScalarGridSpec(
             num_scalar_prefetch=1, grid=grid, in_specs=in_specs, out_specs=out_specs, scratch_shapes=scratch
         ),
-        out_shape=[pltpu.HBM(s.shape, s.dtype) for s in out_shape],
+        out_shape=[pltpu.HBM(s.shape, s.dtype) if k >= free else s for k, s in enumerate(out_shape)],
         compiler_params=pltpu.CompilerParams(vmem_limit_bytes=mib * 2**20),
         cost_estimate=pl.CostEstimate(flops=flops, bytes_accessed=moved, transcendentals=0),
         name=name,
@@ -90,6 +90,7 @@
         10,
         0,
         10 * n * rows * own,
+        1,
     )(jnp.stack(ids + wanted), *parts, gain)
 
 
@@ -255,10 +256,12 @@
     got_z = shift(pieces[1, 2], "zh", 1, 2)
     got_p = shift(after(pieces[1, 1], down, up), "y", 1, 4)
     got_m = shift(after(pieces[1, 3], down, up), "y", 3, 4)
-    near_p = shift(after(pieces[0, 1], got_p, got_m), "y", 1, 4)
-    near_m = shift(after(pieces[0, 3], got_p, got_m), "y", 3, 4)
-    far = shift((pieces[0, 2].astype(f32) + got_z.astype(f32)).astype(bf16), "y", 2, 4)
-    across = shift((pieces[1, 0].astype(f32) + got_p.astype(f32) + got_m.astype(f32)).astype(bf16), "zh", 1, 2)
+    near_p = shift(after(pieces[0, 1], down, up), "y", 1, 4)
+    near_m = shift(after(pieces[0, 3], down, up), "y", 3, 4)
+    far_sent = (pieces[0, 2].astype(f32) + got_z.astype(f32)).astype(bf16)
+    far = shift(far_sent, "y", 2, 4)
+    across_sent = (pieces[1, 0].astype(f32) + got_p.astype(f32) + got_m.astype(f32)).astype(bf16)
+    across = shift(across_sent, "zh", 1, 2)
 
     far_low = shift(after(low[:cut], pieces[0, 0]), "x", 1, 4)
     far_high = shift(after(high[cut:], pieces[0, 0]), "x", 3, 4)
@@ -267,16 +270,24 @@
     rows = own // 2
     sides = [zl ^ 1 ^ parity, zl ^ parity] * 2
     cores = [1 - c, 1 - c, c, c]
-    weight_parts = []
-    got = None
-    for half in (0, 1):
-        sent, kept = outer(same, crossed, grads, half, hidden // 2, sides, cores, rows)
-        got_c = shift(sent, "c", 1, 2)
-        if got is not None:
-            got_c = after(got_c, got)
-        got = shift((kept[:rows] + got_c[:rows].astype(f32)).astype(bf16), "zl", 1, 2)
-        weight_parts.append((kept[rows:] + got_c[rows:].astype(f32)) + got.astype(f32))
-    weight_grad = jnp.concatenate(weight_parts, 1)
+    def pair(value, axis, step, size):
+        return value + shift(value, axis, step, size)
+
+    def send_late(kept, got_c):
+        late = (kept[:rows] + got_c[:rows].astype(f32)).astype(bf16)
+        return late, shift(late, "zl", 1, 2)
+
+    width = hidden // 2
+    sent_a, kept_a = outer(same, crossed, [after(pre_grad, far_sent)] + grads[1:], 0, width, sides, cores, rows)
+    got_ca = shift(after(sent_a, got_p, got_m), "c", 1, 2)
+    ready = after(pre_grad, sent_a)
+    sent_b, kept_b = outer(same, crossed, [ready] + grads[1:], 1, width, sides, cores, rows)
+    late, got_a = send_late(kept_a, after(got_ca, across, sent_b))
+    got_cb = shift(sent_b, "c", 1, 2)
+    late, got_b = send_late(kept_b, after(got_cb, got_a))
+    weight_a = kept_a[rows:] + got_ca[rows:].astype(f32) + got_a.astype(f32)
+    weight_b = kept_b[rows:] + got_cb[rows:].astype(f32) + got_b.astype(f32)
+    weight_grad = jnp.concatenate([weight_a, weight_b], 1)
 
     mean, inv = mean[:, :1], inv[:, :1]
     scaled_own = (inputs.astype(f32) - mean) * inv
@@ -286,14 +297,14 @@
         dnorm = dnorm + value.astype(f32)
     dxhat = dnorm * gain_own
     sums = jnp.stack([jnp.sum(dxhat, axis=1), jnp.sum(dxhat * scaled_own, axis=1)])
-    for axis, step, size in (("zh", 1, 2), ("y", 2, 4), ("y", 1, 4)):
-        sums = sums + shift(sums, axis, step, size)
-    sums = sums * (1.0 / (own * 8))
+    gain_grad = jnp.sum(dnorm * scaled_own, axis=0)
+
+    sums = pair(pair(sums, "y", 2, 4), "zh", 1, 2)
+    gain_grad = pair(pair(pair(gain_grad, "c", 1, 2), "x", 2, 4), "zl", 1, 2)
+    sums = pair(after(sums, late), "y", 1, 4) * (1.0 / (own * 8))
+    gain_grad = pair(after(gain_grad, late), "x", 1, 4)
     first_mean, second_mean = sums[0][:, None], sums[1][:, None]
     input_grad = (out_grad.astype(f32) + inv * (dxhat - first_mean - scaled_own * second_mean)).astype(bf16)
-    gain_grad = jnp.sum(dnorm * scaled_own, axis=0)
-    for axis, step, size in (("c", 1, 2), ("zl", 1, 2), ("x", 2, 4), ("x", 1, 4)):
-        gain_grad = gain_grad + shift(gain_grad, axis, step, size)
     return (input_grad, weight_grad, gain_grad)
 
 

time: 160 us -> 153 us (0.956)
  waiting for transfers between devices: 62.3 us -> 42.6 us
  starting transfers between devices: 40.1 us -> 53.7 us
    ppermute x34, waiting for transfers between devices: 62.3 us -> 42.6 us  [shift(): lax.ppermute(value, axis, [(i, (i + step) % size) for i in range(size)])]
    ppermute x34, starting transfers between devices: 40.1 us -> 53.7 us  [shift(): lax.ppermute(value, axis, [(i, (i + step) % size) for i in range(size)])]
    unnamed x60 -> x56, local copies, waits for them, and re-layouts: 3.74 us -> 2.78 us
  transfers between devices with their start and end apart: 34 -> 34, of which waited for: 18 -> 13; matrix products, arithmetic and copies ran while one was open for 3% -> 3% of each run, Pallas kernels for 24% -> 25%
where the time goes in v3:
time: 153 us; the launch traced here: 151 us
  starting transfers between devices  53.7 us (35%)
  Pallas kernels  44.5 us (29%)
  waiting for transfers between devices  42.6 us (28%)
  other arithmetic  5.17 us (3%)
  local copies, waits for them, and re-layouts  4.1 us (3%)
    ppermute x34, starting transfers between devices, shift(): lax.ppermute(value, axis, [(i, (i + step) % size) for i in range(size)])  53.7 us
    ppermute x34, waiting for transfers between devices, shift(): lax.ppermute(value, axis, [(i, (i + step) % size) for i in range(size)])  42.6 us
    pallas_call x4, Pallas kernels, call(): return lambda ids, *operands: step(ids, *map(in_hbm, operands))  35.8 us
    pallas_call x1, Pallas kernels, project(): pl.pallas_call(kernel, grid=(1,), in_specs=[pl.BlockSpec(normed.shape, la...  8.67 us
  transfers between devices with their start and end apart: 34, of which 13 were waited for; matrix products, arithmetic and copies ran while one was open for 3% of the time, Pallas kernels for 25%

profile of v3, /device:TPU:24, one launch (start us, length us, event | category | flops | bytes accessed | tf_op | source)
XLA Modules:
  0.0 151.1 jit_solution(6630215871098366617)
XLA Ops:
  1.9 3.9 %collective-permute-start = (bf16[256,768]{1,0:T(8,128)(2,1)}, bf16[256,768]{1,0:T(8,128)(2,1)S(1)}, u32[]{:S(2)}, u32[]{:S(2)}) collective-permute-start(bf16[256,768]{1,0:T(8,128)(2,1)} %refs_0_.1), channel_id=1, source_target_pairs={{0,4},{4,0},{1,5},{5,1},{2,6},{6,2},{3,7},{7,3},{8,12},{12,8},{9,1... | collective-permute-start | bytes 1179656 | tf_op jit(solution)/shard_map/ppermute | solution.py:23
  5.8 3.2 %collective-permute-start.2 = (bf16[256,768]{1,0:T(8,128)(2,1)}, bf16[256,768]{1,0:T(8,128)(2,1)S(1)}, u32[]{:S(2)}, u32[]{:S(2)}) collective-permute-start(bf16[256,768]{1,0:T(8,128)(2,1)} %refs_0_.1), channel_id=1, source_target_pairs={{0,1},{1,2},{2,3},{3,0},{4,5},{5,6},{6,7},{7,4},{8,9},{9,10},{10,1... | collective-permute-start | bytes 1179656 | tf_op jit(solution)/shard_map/ppermute | solution.py:23
  9.1 5.4 %collective-permute-done.1.refs_2_ = bf16[256,768]{1,0:T(8,128)(2,1)S(1)} collective-permute-done((bf16[256,768]{1,0:T(8,128)(2,1)}, bf16[256,768]{1,0:T(8,128)(2,1)S(1)}, u32[]{:S(2)}, u32[]{:S(2)}) %collective-permute-start.1) | collective-permute-done | bytes 393248 | tf_op jit(solution)/shard_map/ppermute | solution.py:23
  14.5 3.9 %collective-permute-start.4 = (bf16[256,768]{1,0:T(8,128)(2,1)S(1)}, bf16[256,768]{1,0:T(8,128)(2,1)S(1)}, u32[]{:S(2)}, u32[]{:S(2)}) collective-permute-start(bf16[256,768]{1,0:T(8,128)(2,1)S(1)} %collective-permute-done.1.refs_2_), channel_id=1, source_target_pairs={{0,4},{4,0},{1,5},{5,1},{2,6},{6,2},{3,7},{7,3},{8,12},{12,8},{9,1... | collective-permute-start | bytes 1179656 | tf_op jit(solution)/shard_map/ppermute | solution.py:23
  19.1 2.5 %collective-permute-start.5 = (bf16[256,768]{1,0:T(8,128)(2,1)S(1)}, bf16[256,768]{1,0:T(8,128)(2,1)S(1)}, u32[]{:S(2)}, u32[]{:S(2)}) collective-permute-start(bf16[256,768]{1,0:T(8,128)(2,1)S(1)} %collective-permute-done.refs_1_), channel_id=1, source_target_pairs={{0,1},{1,2},{2,3},{3,0},{4,5},{5,6},{6,7},{7,4},{8,9},{9,10},{10,1... | collective-permute-start | bytes 1179656 | tf_op jit(solution)/shard_map/ppermute | solution.py:23
  21.8 3.6 %collective-permute-done.4.refs_5_ = bf16[256,768]{1,0:T(8,128)(2,1)S(1)} collective-permute-done((bf16[256,768]{1,0:T(8,128)(2,1)S(1)}, bf16[256,768]{1,0:T(8,128)(2,1)S(1)}, u32[]{:S(2)}, u32[]{:S(2)}) %collective-permute-start.4) | collective-permute-done | bytes 393248 | tf_op jit(solution)/shard_map/ppermute | solution.py:23
  25.4 4.7 %collective-permute-done.6.refs_7_ = bf16[256,768]{1,0:T(8,128)(2,1)S(1)} collective-permute-done((bf16[256,768]{1,0:T(8,128)(2,1)S(1)}, bf16[256,768]{1,0:T(8,128)(2,1)S(1)}, u32[]{:S(2)}, u32[]{:S(2)}) %collective-permute-start.6) | collective-permute-done | bytes 393248 | tf_op jit(solution)/shard_map/ppermute | solution.py:23
  31.0 6.4 %normalise.1 = (bf16[256,6144]{1,0:T(8,128)(2,1)S(1)}, f32[256,128]{1,0:T(8,128)}, f32[256,128]{1,0:T(8,128)}, bf16[256,768]{1,0:T(8,128)(2,1)}, bf16[256,768]{1...) custom-call(s32[13]{0:T(128)S(1)} %stack.103.ids_ref, ...), custom_call_target="tpu_custom_call" | custom-call | bytes 15728640 | tf_op jit(solution)/shard_map/normalise/pallas_call | solution.py:45
  39.0 2.7 %collective-permute-start.8 = (bf16[256,768]{1,0:T(8,128)(2,1)}, bf16[256,768]{1,0:T(8,128)(2,1)S(1)}, u32[]{:S(2)}, u32[]{:S(2)}) collective-permute-start(bf16[256,768]{1,0:T(8,128)(2,1)} %get-tuple-element.42), channel_id=1, source_target_pairs={{0,64},{32,96},{64,0},{96,32},{1,65},{33,97},{65,1},{97,33},{2,66}... | collective-permute-start | bytes 1179656 | tf_op jit(solution)/shard_map/ppermute | solution.py:23
  43.1 8.7 %project.1.grad_ref.refs_7_ = bf16[256,1536]{1,0:T(8,128)(2,1)S(1)} custom-call(bf16[256,6144]{1,0:T(8,128)(2,1)S(1)} %get-tuple-element.38.normed_ref, bf16[6144,1536]{1,0:T(8,128)(2,1)} %w_ref.3, bf16[256,1536]{1,0:T(8,128)(2,1)S(1)} %copy-done.1), custom_call_target="tpu_custom_call" | custom-call | flops 4831838208 | bytes 18874368 | tf_op jit(solution)/shard_map/project/pallas_call | solution.py:112
  53.9 6.5 %collective-permute-done.8.refs_3_ = bf16[256,768]{1,0:T(8,128)(2,1)S(1)} collective-permute-done((bf16[256,768]{1,0:T(8,128)(2,1)}, bf16[256,768]{1,0:T(8,128)(2,1)S(1)}, u32[]{:S(2)}, u32[]{:S(2)}) %collective-permute-start.8) | collective-permute-done | bytes 393248 | tf_op jit(solution)/shard_map/ppermute | solution.py:23
  61.3 2.9 %collective-permute-start.11 = (bf16[384,768]{1,0:T(8,128)(2,1)S(1)}, bf16[384,768]{1,0:T(8,128)(2,1)}, u32[]{:S(2)}, u32[]{:S(2)}) collective-permute-start(bf16[384,768]{1,0:T(8,128)(2,1)S(1)} %pad_maximum_fusion.2), channel_id=1, source_target_pairs={{0,1},{1,2},{2,3},{3,0},{4,5},{5,6},{6,7},{7,4},{8,9},{9,10},{10,1... | collective-permute-start | bytes 1769480 | tf_op jit(solution)/shard_map/ppermute | solution.py:23
  64.2 12.2 %spread.1 = (bf16[256,768]{1,0:T(8,128)(2,1)}, bf16[256,768]{1,0:T(8,128)(2,1)}, bf16[256,768]{1,0:T(8,128)(2,1)}, bf16[256,768]{1,0:T(8,128)(2,1)}, bf16[256,76...) custom-call(s32[8]{0:T(128)S(1)} %stack.104.ids_ref, ...), custom_call_target="tpu_custom_call" | custom-call | flops 4831838208 | bytes 18874368 | tf_op jit(solution)/shard_map/spread/pallas_call | solution.py:45
  76.4 3.9 %collective-permute-start.14 = (bf16[256,768]{1,0:T(8,128)(2,1)}, bf16[256,768]{1,0:T(8,128)(2,1)S(1)}, u32[]{:S(2)}, u32[]{:S(2)}) collective-permute-start(bf16[256,768]{1,0:T(8,128)(2,1)} %get-tuple-element.49), channel_id=1, source_target_pairs={{0,4},{4,0},{1,5},{5,1},{2,6},{6,2},{3,7},{7,3},{8,12},{12,8},{9,1... | collective-permute-start | bytes 1179656 | tf_op jit(solution)/shard_map/ppermute | solution.py:23
  81.4 2.3 %collective-permute-start.24 = (bf16[128,1536]{1,0:T(8,128)(2,1)S(1)}, bf16[128,1536]{1,0:T(8,128)(2,1)S(1)}, u32[]{:S(2)}, u32[]{:S(2)}) collective-permute-start(bf16[128,1536]{1,0:T(8,128)(2,1)S(1)} %slice.65), channel_id=1, source_target_pairs={{0,96},{32,0},{64,32},{96,64},{1,97},{33,1},{65,33},{97,65},{2,98}... | collective-permute-start | bytes 1179656 | tf_op jit(solution)/shard_map/ppermute | solution.py:23
  83.9 3.2 %collective-permute-start.16 = (bf16[256,768]{1,0:T(8,128)(2,1)}, bf16[256,768]{1,0:T(8,128)(2,1)S(1)}, u32[]{:S(2)}, u32[]{:S(2)}) collective-permute-start(bf16[256,768]{1,0:T(8,128)(2,1)} %get-tuple-element.52), channel_id=1, source_target_pairs={{0,1},{1,2},{2,3},{3,0},{4,5},{5,6},{6,7},{7,4},{8,9},{9,10},{10,1... | collective-permute-start | bytes 1179656 | tf_op jit(solution)/shard_map/ppermute | solution.py:23
  87.6 2.5 %collective-permute-done.23.refs_10_ = bf16[128,1536]{1,0:T(8,128)(2,1)S(1)} collective-permute-done((bf16[128,1536]{1,0:T(8,128)(2,1)S(1)}, bf16[128,1536]{1,0:T(8,128)(2,1)S(1)}, u32[]{:S(2)}, u32[]{:S(2)}) %collective-permute-start.23) | collective-permute-done | bytes 393248 | tf_op jit(solution)/shard_map/ppermute | solution.py:23
  91.0 8.6 %outer.2 = (bf16[768,768]{1,0:T(8,128)(2,1)}, f32[768,768]{1,0:T(8,128)}) custom-call(s32[8]{0:T(128)S(1)} %stack.112.ids_ref, bf16[256,768]{1,0:T(8,128)(2,1)} %get-tuple-element.56.refs_0_, bf16[256,768]{1,0:T(8,128)(2,1)} %copy-done.6, bf16[256,768]{1,0:T(8,128)(2,1)} %copy-done.7, bf16[256,768]{1,0:T(8,128)(2,1)} %copy-done.5, ...), custom_call_target="tpu_custom_call" | custom-call | flops 2415919104 | bytes 6291456 | tf_op jit(solution)/shard_map/outer/pallas_call | solution.py:45
  99.9 2.4 %collective-permute-start.18 = (bf16[256,768]{1,0:T(8,128)(2,1)S(1)}, bf16[256,768]{1,0:T(8,128)(2,1)S(1)}, u32[]{:S(2)}, u32[]{:S(2)}) collective-permute-start(bf16[256,768]{1,0:T(8,128)(2,1)S(1)} %add_convert_fusion.3), channel_id=1, source_target_pairs={{0,4},{4,0},{1,5},{5,1},{2,6},{6,2},{3,7},{7,3},{8,12},{12,8},{9,1... | collective-permute-start | bytes 1179656 | tf_op jit(solution)/shard_map/ppermute | solution.py:23
  104.5 3.2 %collective-permute-start.12 = (bf16[256,768]{1,0:T(8,128)(2,1)S(1)}, bf16[256,768]{1,0:T(8,128)(2,1)S(1)}, u32[]{:S(2)}, u32[]{:S(2)}) collective-permute-start(bf16[256,768]{1,0:T(8,128)(2,1)S(1)} %copy-done.24), channel_id=1, source_target_pairs={{0,1},{1,2},{2,3},{3,0},{4,5},{5,6},{6,7},{7,4},{8,9},{9,10},{10,1... | collective-permute-start | bytes 1179656 | tf_op jit(solution)/shard_map/ppermute | solution.py:23
  107.7 8.6 %outer.3 = (bf16[768,768]{1,0:T(8,128)(2,1)}, f32[768,768]{1,0:T(8,128)}) custom-call(s32[8]{0:T(128)S(1)} %stack.112.ids_ref, bf16[256,768]{1,0:T(8,128)(2,1)} %get-tuple-element.56.refs_0_, bf16[256,768]{1,0:T(8,128)(2,1)} %copy-done.6, bf16[256,768]{1,0:T(8,128)(2,1)} %copy-done.7, bf16[256,768]{1,0:T(8,128)(2,1)} %copy-done.5, ...), custom_call_target="tpu_custom_call" | custom-call | flops 2415919104 | bytes 6291456 | tf_op jit(solution)/shard_map/outer/pallas_call | solution.py:45
  117.8 6.6 %collective-permute-done.13 = bf16[256,768]{1,0:T(8,128)(2,1)S(1)} collective-permute-done((bf16[256,768]{1,0:T(8,128)(2,1)S(1)}, bf16[256,768]{1,0:T(8,128)(2,1)S(1)}, u32[]{:S(2)}, u32[]{:S(2)}) %collective-permute-start.13) | collective-permute-done | bytes 393248 | tf_op jit(solution)/shard_map/ppermute | solution.py:23
  132.7 2.9 %collective-permute-done.20 = f32[2,256]{1,0:T(2,128)S(1)} collective-permute-done((f32[2,256]{1,0:T(2,128)S(1)}, f32[2,256]{1,0:T(2,128)S(1)}, u32[]{:S(2)}, u32[]{:S(2)}) %collective-permute-start.20) | collective-permute-done | bytes 2080 | tf_op jit(solution)/shard_map/ppermute | solution.py:23
  144.0 5.2 %collective-permute-done.29 = bf16[384,768]{1,0:T(8,128)(2,1)S(1)} collective-permute-done((bf16[384,768]{1,0:T(8,128)(2,1)S(1)}, bf16[384,768]{1,0:T(8,128)(2,1)S(1)}, u32[]{:S(2)}, u32[]{:S(2)}) %collective-permute-start.29) | collective-permute-done | bytes 589856 | tf_op jit(solution)/shard_map/ppermute | solution.py:23
  (134 shorter events, 34.1 us)
Async XLA Ops:
  0.6 13.8 %collective-permute-start.1 = (bf16[256,768]{1,0:T(8,128)(2,1)}, bf16[256,768]{1,0:T(8,128)(2,1)S(1)}, u32[]{:S(2)}, u32[]{:S(2)}) collective-permute-start(bf16[256,768]{1,0:T(8,128)(2,1)} %refs_0_.1), channel_id=1, source_target_pairs={{0,2},{1,3},{2,0},{3,1},{4,6},{5,7},{6,4},{7,5},{8,10},{9,11},{10,... | collective-permute-start | bytes 1179656 | tf_op jit(solution)/shard_map/ppermute | solution.py:23
  1.9 16.4 %collective-permute-start = (bf16[256,768]{1,0:T(8,128)(2,1)}, bf16[256,768]{1,0:T(8,128)(2,1)S(1)}, u32[]{:S(2)}, u32[]{:S(2)}) collective-permute-start(bf16[256,768]{1,0:T(8,128)(2,1)} %refs_0_.1), channel_id=1, source_target_pairs={{0,4},{4,0},{1,5},{5,1},{2,6},{6,2},{3,7},{7,3},{8,12},{12,8},{9,1... | collective-permute-start | bytes 1179656 | tf_op jit(solution)/shard_map/ppermute | solution.py:23
  5.8 16.0 %collective-permute-start.3 = (bf16[256,768]{1,0:T(8,128)(2,1)}, bf16[256,768]{1,0:T(8,128)(2,1)S(1)}, u32[]{:S(2)}, u32[]{:S(2)}) collective-permute-start(bf16[256,768]{1,0:T(8,128)(2,1)} %refs_0_.1), channel_id=1, source_target_pairs={{0,3},{1,0},{2,1},{3,2},{4,7},{5,4},{6,5},{7,6},{8,11},{9,8},{10,9... | collective-permute-start | bytes 1179656 | tf_op jit(solution)/shard_map/ppermute | solution.py:23
  5.8 16.0 %collective-permute-start.2 = (bf16[256,768]{1,0:T(8,128)(2,1)}, bf16[256,768]{1,0:T(8,128)(2,1)S(1)}, u32[]{:S(2)}, u32[]{:S(2)}) collective-permute-start(bf16[256,768]{1,0:T(8,128)(2,1)} %refs_0_.1), channel_id=1, source_target_pairs={{0,1},{1,2},{2,3},{3,0},{4,5},{5,6},{6,7},{7,4},{8,9},{9,10},{10,1... | collective-permute-start | bytes 1179656 | tf_op jit(solution)/shard_map/ppermute | solution.py:23
  18.4 11.8 %collective-permute-start.6 = (bf16[256,768]{1,0:T(8,128)(2,1)S(1)}, bf16[256,768]{1,0:T(8,128)(2,1)S(1)}, u32[]{:S(2)}, u32[]{:S(2)}) collective-permute-start(bf16[256,768]{1,0:T(8,128)(2,1)S(1)} %collective-permute-done.refs_1_), channel_id=1, source_target_pairs={{0,3},{1,0},{2,1},{3,2},{4,7},{5,4},{6,5},{7,6},{8,11},{9,8},{10,9... | collective-permute-start | bytes 1179656 | tf_op jit(solution)/shard_map/ppermute | solution.py:23
  19.1 11.0 %collective-permute-start.5 = (bf16[256,768]{1,0:T(8,128)(2,1)S(1)}, bf16[256,768]{1,0:T(8,128)(2,1)S(1)}, u32[]{:S(2)}, u32[]{:S(2)}) collective-permute-start(bf16[256,768]{1,0:T(8,128)(2,1)S(1)} %collective-permute-done.refs_1_), channel_id=1, source_target_pairs={{0,1},{1,2},{2,3},{3,0},{4,5},{5,6},{6,7},{7,4},{8,9},{9,10},{10,1... | collective-permute-start | bytes 1179656 | tf_op jit(solution)/shard_map/ppermute | solution.py:23
  37.4 23.0 %collective-permute-start.7 = (bf16[256,768]{1,0:T(8,128)(2,1)}, bf16[256,768]{1,0:T(8,128)(2,1)S(1)}, u32[]{:S(2)}, u32[]{:S(2)}) collective-permute-start(bf16[256,768]{1,0:T(8,128)(2,1)} %get-tuple-element.41), channel_id=1, source_target_pairs={{0,32},{32,64},{64,96},{96,0},{1,33},{33,65},{65,97},{97,1},{2,34}... | collective-permute-start | bytes 1179656 | tf_op jit(solution)/shard_map/ppermute | solution.py:23
  39.0 21.4 %collective-permute-start.8 = (bf16[256,768]{1,0:T(8,128)(2,1)}, bf16[256,768]{1,0:T(8,128)(2,1)S(1)}, u32[]{:S(2)}, u32[]{:S(2)}) collective-permute-start(bf16[256,768]{1,0:T(8,128)(2,1)} %get-tuple-element.42), channel_id=1, source_target_pairs={{0,64},{32,96},{64,0},{96,32},{1,65},{33,97},{65,1},{97,33},{2,66}... | collective-permute-start | bytes 1179656 | tf_op jit(solution)/shard_map/ppermute | solution.py:23
  41.7 19.5 %collective-permute-start.10 = (bf16[256,768]{1,0:T(8,128)(2,1)}, bf16[256,768]{1,0:T(8,128)(2,1)S(1)}, u32[]{:S(2)}, u32[]{:S(2)}) collective-permute-start(bf16[256,768]{1,0:T(8,128)(2,1)} %get-tuple-element.44), channel_id=1, source_target_pairs={{0,96},{32,0},{64,32},{96,64},{1,97},{33,1},{65,33},{97,65},{2,98}... | collective-permute-start | bytes 1179656 | tf_op jit(solution)/shard_map/ppermute | solution.py:23
  51.8 28.5 %collective-permute-start.22 = (bf16[256,1536]{1,0:T(8,128)(2,1)S(1)}, bf16[256,1536]{1,0:T(8,128)(2,1)S(1)}, u32[]{:S(2)}, u32[]{:S(2)}) collective-permute-start(bf16[256,1536]{1,0:T(8,128)(2,1)S(1)} %project.1.grad_ref.refs_7_), channel_id=1, source_target_pairs={{0,96},{32,0},{64,32},{96,64},{1,97},{33,1},{65,33},{97,65},{2,98}... | collective-permute-start | bytes 2359304 | tf_op jit(solution)/shard_map/ppermute | solution.py:23
  51.9 28.4 %collective-permute-start.21 = (bf16[256,1536]{1,0:T(8,128)(2,1)S(1)}, bf16[256,1536]{1,0:T(8,128)(2,1)S(1)}, u32[]{:S(2)}, u32[]{:S(2)}) collective-permute-start(bf16[256,1536]{1,0:T(8,128)(2,1)S(1)} %project.1.grad_ref.refs_7_), channel_id=1, source_target_pairs={{0,32},{32,64},{64,96},{96,0},{1,33},{33,65},{65,97},{97,1},{2,34}... | collective-permute-start | bytes 2359304 | tf_op jit(solution)/shard_map/ppermute | solution.py:23
  60.5 23.3 %collective-permute-start.9 = (bf16[384,768]{1,0:T(8,128)(2,1)S(1)}, bf16[384,768]{1,0:T(8,128)(2,1)}, u32[]{:S(2)}, u32[]{:S(2)}) collective-permute-start(bf16[384,768]{1,0:T(8,128)(2,1)S(1)} %pad_maximum_fusion.1), channel_id=1, source_target_pairs={{0,3},{1,0},{2,1},{3,2},{4,7},{5,4},{6,5},{7,6},{8,11},{9,8},{10,9... | collective-permute-start | bytes 1769480 | tf_op jit(solution)/shard_map/ppermute | solution.py:23
  61.3 22.5 %collective-permute-start.11 = (bf16[384,768]{1,0:T(8,128)(2,1)S(1)}, bf16[384,768]{1,0:T(8,128)(2,1)}, u32[]{:S(2)}, u32[]{:S(2)}) collective-permute-start(bf16[384,768]{1,0:T(8,128)(2,1)S(1)} %pad_maximum_fusion.2), channel_id=1, source_target_pairs={{0,1},{1,2},{2,3},{3,0},{4,5},{5,6},{6,7},{7,4},{8,9},{9,10},{10,1... | collective-permute-start | bytes 1769480 | tf_op jit(solution)/shard_map/ppermute | solution.py:23
  76.4 11.0 %collective-permute-start.14 = (bf16[256,768]{1,0:T(8,128)(2,1)}, bf16[256,768]{1,0:T(8,128)(2,1)S(1)}, u32[]{:S(2)}, u32[]{:S(2)}) collective-permute-start(bf16[256,768]{1,0:T(8,128)(2,1)} %get-tuple-element.49), channel_id=1, source_target_pairs={{0,4},{4,0},{1,5},{5,1},{2,6},{6,2},{3,7},{7,3},{8,12},{12,8},{9,1... | collective-permute-start | bytes 1179656 | tf_op jit(solution)/shard_map/ppermute | solution.py:23
  83.8 15.8 %collective-permute-start.17 = (bf16[256,768]{1,0:T(8,128)(2,1)}, bf16[256,768]{1,0:T(8,128)(2,1)S(1)}, u32[]{:S(2)}, u32[]{:S(2)}) collective-permute-start(bf16[256,768]{1,0:T(8,128)(2,1)} %get-tuple-element.54), channel_id=1, source_target_pairs={{0,3},{1,0},{2,1},{3,2},{4,7},{5,4},{6,5},{7,6},{8,11},{9,8},{10,9... | collective-permute-start | bytes 1179656 | tf_op jit(solution)/shard_map/ppermute | solution.py:23
  83.9 15.7 %collective-permute-start.16 = (bf16[256,768]{1,0:T(8,128)(2,1)}, bf16[256,768]{1,0:T(8,128)(2,1)S(1)}, u32[]{:S(2)}, u32[]{:S(2)}) collective-permute-start(bf16[256,768]{1,0:T(8,128)(2,1)} %get-tuple-element.52), channel_id=1, source_target_pairs={{0,1},{1,2},{2,3},{3,0},{4,5},{5,6},{6,7},{7,4},{8,9},{9,10},{10,1... | collective-permute-start | bytes 1179656 | tf_op jit(solution)/shard_map/ppermute | solution.py:23
  99.6 16.9 %collective-permute-start.26 = (bf16[768,768]{1,0:T(8,128)(2,1)}, bf16[768,768]{1,0:T(8,128)(2,1)S(1)}, u32[]{:S(2)}, u32[]{:S(2)}) collective-permute-start(bf16[768,768]{1,0:T(8,128)(2,1)} %get-tuple-element.66), channel_id=1, source_target_pairs={{0,8},{8,0},{1,9},{9,1},{2,10},{10,2},{3,11},{11,3},{4,12},{12,4},... | collective-permute-start | bytes 3538952 | tf_op jit(solution)/shard_map/ppermute | solution.py:23
  99.9 16.4 %collective-permute-start.18 = (bf16[256,768]{1,0:T(8,128)(2,1)S(1)}, bf16[256,768]{1,0:T(8,128)(2,1)S(1)}, u32[]{:S(2)}, u32[]{:S(2)}) collective-permute-start(bf16[256,768]{1,0:T(8,128)(2,1)S(1)} %add_convert_fusion.3), channel_id=1, source_target_pairs={{0,4},{4,0},{1,5},{5,1},{2,6},{6,2},{3,7},{7,3},{8,12},{12,8},{9,1... | collective-permute-start | bytes 1179656 | tf_op jit(solution)/shard_map/ppermute | solution.py:23
  103.2 14.7 %collective-permute-start.15 = (bf16[256,768]{1,0:T(8,128)(2,1)S(1)}, bf16[256,768]{1,0:T(8,128)(2,1)S(1)}, u32[]{:S(2)}, u32[]{:S(2)}) collective-permute-start(bf16[256,768]{1,0:T(8,128)(2,1)S(1)} %add_convert_fusion.4), channel_id=1, source_target_pairs={{0,2},{1,3},{2,0},{3,1},{4,6},{5,7},{6,4},{7,5},{8,10},{9,11},{10,... | collective-permute-start | bytes 1179656 | tf_op jit(solution)/shard_map/ppermute | solution.py:23
  104.5 19.9 %collective-permute-start.13 = (bf16[256,768]{1,0:T(8,128)(2,1)S(1)}, bf16[256,768]{1,0:T(8,128)(2,1)S(1)}, u32[]{:S(2)}, u32[]{:S(2)}) collective-permute-start(bf16[256,768]{1,0:T(8,128)(2,1)S(1)} %copy-done.25), channel_id=1, source_target_pairs={{0,3},{1,0},{2,1},{3,2},{4,7},{5,4},{6,5},{7,6},{8,11},{9,8},{10,9... | collective-permute-start | bytes 1179656 | tf_op jit(solution)/shard_map/ppermute | solution.py:23
  104.5 19.9 %collective-permute-start.12 = (bf16[256,768]{1,0:T(8,128)(2,1)S(1)}, bf16[256,768]{1,0:T(8,128)(2,1)S(1)}, u32[]{:S(2)}, u32[]{:S(2)}) collective-permute-start(bf16[256,768]{1,0:T(8,128)(2,1)S(1)} %copy-done.24), channel_id=1, source_target_pairs={{0,1},{1,2},{2,3},{3,0},{4,5},{5,6},{6,7},{7,4},{8,9},{9,10},{10,1... | collective-permute-start | bytes 1179656 | tf_op jit(solution)/shard_map/ppermute | solution.py:23
  116.3 19.2 %collective-permute-start.25 = (bf16[768,768]{1,0:T(8,128)(2,1)}, bf16[768,768]{1,0:T(8,128)(2,1)S(1)}, u32[]{:S(2)}, u32[]{:S(2)}) collective-permute-start(bf16[768,768]{1,0:T(8,128)(2,1)} %get-tuple-element.64), channel_id=1, source_target_pairs={{0,8},{8,0},{1,9},{9,1},{2,10},{10,2},{3,11},{11,3},{4,12},{12,4},... | collective-permute-start | bytes 3538952 | tf_op jit(solution)/shard_map/ppermute | solution.py:23
  116.7 18.8 %collective-permute-start.27 = (bf16[384,768]{1,0:T(8,128)(2,1)S(1)}, bf16[384,768]{1,0:T(8,128)(2,1)S(1)}, u32[]{:S(2)}, u32[]{:S(2)}) collective-permute-start(bf16[384,768]{1,0:T(8,128)(2,1)S(1)} %add_convert_fusion.1), channel_id=1, source_target_pairs={{0,16},{16,0},{1,17},{17,1},{2,18},{18,2},{3,19},{19,3},{4,20},{20... | collective-permute-start | bytes 1769480 | tf_op jit(solution)/shard_map/ppermute | solution.py:23
  135.8 13.4 %collective-permute-start.29 = (bf16[384,768]{1,0:T(8,128)(2,1)S(1)}, bf16[384,768]{1,0:T(8,128)(2,1)S(1)}, u32[]{:S(2)}, u32[]{:S(2)}) collective-permute-start(bf16[384,768]{1,0:T(8,128)(2,1)S(1)} %add_convert_fusion), channel_id=1, source_target_pairs={{0,16},{16,0},{1,17},{17,1},{2,18},{18,2},{3,19},{19,3},{4,20},{20... | collective-permute-start | bytes 1769480 | tf_op jit(solution)/shard_map/ppermute | solution.py:23
  (38 other events, 255.3 us)

commit v4 on v3

--- a/solution.py
+++ b/solution.py
@@ -300,9 +300,9 @@
     gain_grad = jnp.sum(dnorm * scaled_own, axis=0)
 
     sums = pair(pair(sums, "y", 2, 4), "zh", 1, 2)
-    gain_grad = pair(pair(pair(gain_grad, "c", 1, 2), "x", 2, 4), "zl", 1, 2)
+    gain_grad = pair(pair(gain_grad, "c", 1, 2), "zl", 1, 2)
     sums = pair(after(sums, late), "y", 1, 4) * (1.0 / (own * 8))
-    gain_grad = pair(after(gain_grad, late), "x", 1, 4)
+    gain_grad = pair(pair(after(gain_grad, late), "x", 2, 4), "x", 1, 4)
     first_mean, second_mean = sums[0][:, None], sums[1][:, None]
     input_grad = (out_grad.astype(f32) + inv * (dxhat - first_mean - scaled_own * second_mean)).astype(bf16)
     return (input_grad, weight_grad, gain_grad)

time: 153 us -> 151 us (0.987)
  no operation moved by 1% of the time
where the time goes in v4:
time: 151 us
  starting transfers between devices  52.6 us (35%)
  Pallas kernels  44.5 us (29%)
  waiting for transfers between devices  43.2 us (29%)
  other arithmetic  5.17 us (3%)
  local copies, waits for them, and re-layouts  4.1 us (3%)
    ppermute x34, starting transfers between devices, shift(): lax.ppermute(value, axis, [(i, (i + step) % size) for i in range(size)])  52.6 us
    ppermute x34, waiting for transfers between devices, shift(): lax.ppermute(value, axis, [(i, (i + step) % size) for i in range(size)])  43.2 us
    pallas_call x4, Pallas kernels, call(): return lambda ids, *operands: step(ids, *map(in_hbm, operands))  35.8 us
    pallas_call x1, Pallas kernels, project(): pl.pallas_call(kernel, grid=(1,), in_specs=[pl.BlockSpec(normed.shape, la...  8.67 us
  transfers between devices with their start and end apart: 34, of which 13 were waited for; matrix products, arithmetic and copies ran while one was open for 3% of the time, Pallas kernels for 25%

profile of v4, /device:TPU:24, one launch (start us, length us, event | category | flops | bytes accessed | tf_op | source)
XLA Modules:
  0.0 150.6 jit_solution(16858262370939749404)
XLA Ops:
  1.9 3.9 %collective-permute-start = (bf16[256,768]{1,0:T(8,128)(2,1)}, bf16[256,768]{1,0:T(8,128)(2,1)S(1)}, u32[]{:S(2)}, u32[]{:S(2)}) collective-permute-start(bf16[256,768]{1,0:T(8,128)(2,1)} %refs_0_.1), channel_id=1, source_target_pairs={{0,4},{4,0},{1,5},{5,1},{2,6},{6,2},{3,7},{7,3},{8,12},{12,8},{9,1... | collective-permute-start | bytes 1179656 | tf_op jit(solution)/shard_map/ppermute | solution.py:23
  5.8 3.2 %collective-permute-start.2 = (bf16[256,768]{1,0:T(8,128)(2,1)}, bf16[256,768]{1,0:T(8,128)(2,1)S(1)}, u32[]{:S(2)}, u32[]{:S(2)}) collective-permute-start(bf16[256,768]{1,0:T(8,128)(2,1)} %refs_0_.1), channel_id=1, source_target_pairs={{0,1},{1,2},{2,3},{3,0},{4,5},{5,6},{6,7},{7,4},{8,9},{9,10},{10,1... | collective-permute-start | bytes 1179656 | tf_op jit(solution)/shard_map/ppermute | solution.py:23
  9.1 5.4 %collective-permute-done.1.refs_2_ = bf16[256,768]{1,0:T(8,128)(2,1)S(1)} collective-permute-done((bf16[256,768]{1,0:T(8,128)(2,1)}, bf16[256,768]{1,0:T(8,128)(2,1)S(1)}, u32[]{:S(2)}, u32[]{:S(2)}) %collective-permute-start.1) | collective-permute-done | bytes 393248 | tf_op jit(solution)/shard_map/ppermute | solution.py:23
  14.5 3.9 %collective-permute-start.4 = (bf16[256,768]{1,0:T(8,128)(2,1)S(1)}, bf16[256,768]{1,0:T(8,128)(2,1)S(1)}, u32[]{:S(2)}, u32[]{:S(2)}) collective-permute-start(bf16[256,768]{1,0:T(8,128)(2,1)S(1)} %collective-permute-done.1.refs_2_), channel_id=1, source_target_pairs={{0,4},{4,0},{1,5},{5,1},{2,6},{6,2},{3,7},{7,3},{8,12},{12,8},{9,1... | collective-permute-start | bytes 1179656 | tf_op jit(solution)/shard_map/ppermute | solution.py:23
  19.1 2.5 %collective-permute-start.5 = (bf16[256,768]{1,0:T(8,128)(2,1)S(1)}, bf16[256,768]{1,0:T(8,128)(2,1)S(1)}, u32[]{:S(2)}, u32[]{:S(2)}) collective-permute-start(bf16[256,768]{1,0:T(8,128)(2,1)S(1)} %collective-permute-done.refs_1_), channel_id=1, source_target_pairs={{0,1},{1,2},{2,3},{3,0},{4,5},{5,6},{6,7},{7,4},{8,9},{9,10},{10,1... | collective-permute-start | bytes 1179656 | tf_op jit(solution)/shard_map/ppermute | solution.py:23
  21.8 3.6 %collective-permute-done.4.refs_5_ = bf16[256,768]{1,0:T(8,128)(2,1)S(1)} collective-permute-done((bf16[256,768]{1,0:T(8,128)(2,1)S(1)}, bf16[256,768]{1,0:T(8,128)(2,1)S(1)}, u32[]{:S(2)}, u32[]{:S(2)}) %collective-permute-start.4) | collective-permute-done | bytes 393248 | tf_op jit(solution)/shard_map/ppermute | solution.py:23
  25.4 4.7 %collective-permute-done.6.refs_7_ = bf16[256,768]{1,0:T(8,128)(2,1)S(1)} collective-permute-done((bf16[256,768]{1,0:T(8,128)(2,1)S(1)}, bf16[256,768]{1,0:T(8,128)(2,1)S(1)}, u32[]{:S(2)}, u32[]{:S(2)}) %collective-permute-start.6) | collective-permute-done | bytes 393248 | tf_op jit(solution)/shard_map/ppermute | solution.py:23
  31.0 6.4 %normalise.1 = (bf16[256,6144]{1,0:T(8,128)(2,1)S(1)}, f32[256,128]{1,0:T(8,128)}, f32[256,128]{1,0:T(8,128)}, bf16[256,768]{1,0:T(8,128)(2,1)}, bf16[256,768]{1...) custom-call(s32[13]{0:T(128)S(1)} %stack.103.ids_ref, ...), custom_call_target="tpu_custom_call" | custom-call | bytes 15728640 | tf_op jit(solution)/shard_map/normalise/pallas_call | solution.py:45
  39.0 2.7 %collective-permute-start.8 = (bf16[256,768]{1,0:T(8,128)(2,1)}, bf16[256,768]{1,0:T(8,128)(2,1)S(1)}, u32[]{:S(2)}, u32[]{:S(2)}) collective-permute-start(bf16[256,768]{1,0:T(8,128)(2,1)} %get-tuple-element.42), channel_id=1, source_target_pairs={{0,64},{32,96},{64,0},{96,32},{1,65},{33,97},{65,1},{97,33},{2,66}... | collective-permute-start | bytes 1179656 | tf_op jit(solution)/shard_map/ppermute | solution.py:23
  43.1 8.7 %project.1.grad_ref.refs_7_ = bf16[256,1536]{1,0:T(8,128)(2,1)S(1)} custom-call(bf16[256,6144]{1,0:T(8,128)(2,1)S(1)} %get-tuple-element.38.normed_ref, bf16[6144,1536]{1,0:T(8,128)(2,1)} %w_ref.3, bf16[256,1536]{1,0:T(8,128)(2,1)S(1)} %copy-done.1), custom_call_target="tpu_custom_call" | custom-call | flops 4831838208 | bytes 18874368 | tf_op jit(solution)/shard_map/project/pallas_call | solution.py:112
  53.9 6.5 %collective-permute-done.8.refs_3_ = bf16[256,768]{1,0:T(8,128)(2,1)S(1)} collective-permute-done((bf16[256,768]{1,0:T(8,128)(2,1)}, bf16[256,768]{1,0:T(8,128)(2,1)S(1)}, u32[]{:S(2)}, u32[]{:S(2)}) %collective-permute-start.8) | collective-permute-done | bytes 393248 | tf_op jit(solution)/shard_map/ppermute | solution.py:23
  61.3 2.9 %collective-permute-start.11 = (bf16[384,768]{1,0:T(8,128)(2,1)S(1)}, bf16[384,768]{1,0:T(8,128)(2,1)}, u32[]{:S(2)}, u32[]{:S(2)}) collective-permute-start(bf16[384,768]{1,0:T(8,128)(2,1)S(1)} %pad_maximum_fusion.2), channel_id=1, source_target_pairs={{0,1},{1,2},{2,3},{3,0},{4,5},{5,6},{6,7},{7,4},{8,9},{9,10},{10,1... | collective-permute-start | bytes 1769480 | tf_op jit(solution)/shard_map/ppermute | solution.py:23
  64.2 12.2 %spread.1 = (bf16[256,768]{1,0:T(8,128)(2,1)}, bf16[256,768]{1,0:T(8,128)(2,1)}, bf16[256,768]{1,0:T(8,128)(2,1)}, bf16[256,768]{1,0:T(8,128)(2,1)}, bf16[256,76...) custom-call(s32[8]{0:T(128)S(1)} %stack.104.ids_ref, ...), custom_call_target="tpu_custom_call" | custom-call | flops 4831838208 | bytes 18874368 | tf_op jit(solution)/shard_map/spread/pallas_call | solution.py:45
  76.4 3.9 %collective-permute-start.14 = (bf16[256,768]{1,0:T(8,128)(2,1)}, bf16[256,768]{1,0:T(8,128)(2,1)S(1)}, u32[]{:S(2)}, u32[]{:S(2)}) collective-permute-start(bf16[256,768]{1,0:T(8,128)(2,1)} %get-tuple-element.49), channel_id=1, source_target_pairs={{0,4},{4,0},{1,5},{5,1},{2,6},{6,2},{3,7},{7,3},{8,12},{12,8},{9,1... | collective-permute-start | bytes 1179656 | tf_op jit(solution)/shard_map/ppermute | solution.py:23
  83.9 3.2 %collective-permute-start.16 = (bf16[256,768]{1,0:T(8,128)(2,1)}, bf16[256,768]{1,0:T(8,128)(2,1)S(1)}, u32[]{:S(2)}, u32[]{:S(2)}) collective-permute-start(bf16[256,768]{1,0:T(8,128)(2,1)} %get-tuple-element.52), channel_id=1, source_target_pairs={{0,1},{1,2},{2,3},{3,0},{4,5},{5,6},{6,7},{7,4},{8,9},{9,10},{10,1... | collective-permute-start | bytes 1179656 | tf_op jit(solution)/shard_map/ppermute | solution.py:23
  87.6 2.5 %collective-permute-done.23.refs_10_ = bf16[128,1536]{1,0:T(8,128)(2,1)S(1)} collective-permute-done((bf16[128,1536]{1,0:T(8,128)(2,1)S(1)}, bf16[128,1536]{1,0:T(8,128)(2,1)S(1)}, u32[]{:S(2)}, u32[]{:S(2)}) %collective-permute-start.23) | collective-permute-done | bytes 393248 | tf_op jit(solution)/shard_map/ppermute | solution.py:23
  91.0 8.6 %outer.2 = (bf16[768,768]{1,0:T(8,128)(2,1)}, f32[768,768]{1,0:T(8,128)}) custom-call(s32[8]{0:T(128)S(1)} %stack.112.ids_ref, bf16[256,768]{1,0:T(8,128)(2,1)} %get-tuple-element.56.refs_0_, bf16[256,768]{1,0:T(8,128)(2,1)} %copy-done.6, bf16[256,768]{1,0:T(8,128)(2,1)} %copy-done.7, bf16[256,768]{1,0:T(8,128)(2,1)} %copy-done.5, ...), custom_call_target="tpu_custom_call" | custom-call | flops 2415919104 | bytes 6291456 | tf_op jit(solution)/shard_map/outer/pallas_call | solution.py:45
  99.9 2.4 %collective-permute-start.18 = (bf16[256,768]{1,0:T(8,128)(2,1)S(1)}, bf16[256,768]{1,0:T(8,128)(2,1)S(1)}, u32[]{:S(2)}, u32[]{:S(2)}) collective-permute-start(bf16[256,768]{1,0:T(8,128)(2,1)S(1)} %add_convert_fusion.3), channel_id=1, source_target_pairs={{0,4},{4,0},{1,5},{5,1},{2,6},{6,2},{3,7},{7,3},{8,12},{12,8},{9,1... | collective-permute-start | bytes 1179656 | tf_op jit(solution)/shard_map/ppermute | solution.py:23
  104.5 3.2 %collective-permute-start.12 = (bf16[256,768]{1,0:T(8,128)(2,1)S(1)}, bf16[256,768]{1,0:T(8,128)(2,1)S(1)}, u32[]{:S(2)}, u32[]{:S(2)}) collective-permute-start(bf16[256,768]{1,0:T(8,128)(2,1)S(1)} %copy-done.24), channel_id=1, source_target_pairs={{0,1},{1,2},{2,3},{3,0},{4,5},{5,6},{6,7},{7,4},{8,9},{9,10},{10,1... | collective-permute-start | bytes 1179656 | tf_op jit(solution)/shard_map/ppermute | solution.py:23
  107.7 8.6 %outer.3 = (bf16[768,768]{1,0:T(8,128)(2,1)}, f32[768,768]{1,0:T(8,128)}) custom-call(s32[8]{0:T(128)S(1)} %stack.112.ids_ref, bf16[256,768]{1,0:T(8,128)(2,1)} %get-tuple-element.56.refs_0_, bf16[256,768]{1,0:T(8,128)(2,1)} %copy-done.6, bf16[256,768]{1,0:T(8,128)(2,1)} %copy-done.7, bf16[256,768]{1,0:T(8,128)(2,1)} %copy-done.5, ...), custom_call_target="tpu_custom_call" | custom-call | flops 2415919104 | bytes 6291456 | tf_op jit(solution)/shard_map/outer/pallas_call | solution.py:45
  117.8 6.6 %collective-permute-done.13 = bf16[256,768]{1,0:T(8,128)(2,1)S(1)} collective-permute-done((bf16[256,768]{1,0:T(8,128)(2,1)S(1)}, bf16[256,768]{1,0:T(8,128)(2,1)S(1)}, u32[]{:S(2)}, u32[]{:S(2)}) %collective-permute-start.13) | collective-permute-done | bytes 393248 | tf_op jit(solution)/shard_map/ppermute | solution.py:23
  126.4 3.8 %collective-permute-done.19 = f32[2,256]{1,0:T(2,128)S(1)} collective-permute-done((f32[2,256]{1,0:T(2,128)S(1)}, f32[2,256]{1,0:T(2,128)S(1)}, u32[]{:S(2)}, u32[]{:S(2)}) %collective-permute-start.19) | collective-permute-done | bytes 2080 | tf_op jit(solution)/shard_map/ppermute | solution.py:23
  132.5 2.9 %collective-permute-done.20 = f32[2,256]{1,0:T(2,128)S(1)} collective-permute-done((f32[2,256]{1,0:T(2,128)S(1)}, f32[2,256]{1,0:T(2,128)S(1)}, u32[]{:S(2)}, u32[]{:S(2)}) %collective-permute-start.20) | collective-permute-done | bytes 2080 | tf_op jit(solution)/shard_map/ppermute | solution.py:23
  144.1 3.2 %collective-permute-done.33 = f32[768]{0:T(1024)S(1)} collective-permute-done((f32[768]{0:T(1024)S(1)}, f32[768]{0:T(1024)S(1)}, u32[]{:S(2)}, u32[]{:S(2)}) %collective-permute-start.33) | collective-permute-done | bytes 3104 | tf_op jit(solution)/shard_map/ppermute | solution.py:23
  (134 shorter events, 34.0 us)
Async XLA Ops:
  0.6 13.8 %collective-permute-start.1 = (bf16[256,768]{1,0:T(8,128)(2,1)}, bf16[256,768]{1,0:T(8,128)(2,1)S(1)}, u32[]{:S(2)}, u32[]{:S(2)}) collective-permute-start(bf16[256,768]{1,0:T(8,128)(2,1)} %refs_0_.1), channel_id=1, source_target_pairs={{0,2},{1,3},{2,0},{3,1},{4,6},{5,7},{6,4},{7,5},{8,10},{9,11},{10,... | collective-permute-start | bytes 1179656 | tf_op jit(solution)/shard_map/ppermute | solution.py:23
  1.9 16.4 %collective-permute-start = (bf16[256,768]{1,0:T(8,128)(2,1)}, bf16[256,768]{1,0:T(8,128)(2,1)S(1)}, u32[]{:S(2)}, u32[]{:S(2)}) collective-permute-start(bf16[256,768]{1,0:T(8,128)(2,1)} %refs_0_.1), channel_id=1, source_target_pairs={{0,4},{4,0},{1,5},{5,1},{2,6},{6,2},{3,7},{7,3},{8,12},{12,8},{9,1... | collective-permute-start | bytes 1179656 | tf_op jit(solution)/shard_map/ppermute | solution.py:23
  5.8 16.0 %collective-permute-start.3 = (bf16[256,768]{1,0:T(8,128)(2,1)}, bf16[256,768]{1,0:T(8,128)(2,1)S(1)}, u32[]{:S(2)}, u32[]{:S(2)}) collective-permute-start(bf16[256,768]{1,0:T(8,128)(2,1)} %refs_0_.1), channel_id=1, source_target_pairs={{0,3},{1,0},{2,1},{3,2},{4,7},{5,4},{6,5},{7,6},{8,11},{9,8},{10,9... | collective-permute-start | bytes 1179656 | tf_op jit(solution)/shard_map/ppermute | solution.py:23
  5.8 16.0 %collective-permute-start.2 = (bf16[256,768]{1,0:T(8,128)(2,1)}, bf16[256,768]{1,0:T(8,128)(2,1)S(1)}, u32[]{:S(2)}, u32[]{:S(2)}) collective-permute-start(bf16[256,768]{1,0:T(8,128)(2,1)} %refs_0_.1), channel_id=1, source_target_pairs={{0,1},{1,2},{2,3},{3,0},{4,5},{5,6},{6,7},{7,4},{8,9},{9,10},{10,1... | collective-permute-start | bytes 1179656 | tf_op jit(solution)/shard_map/ppermute | solution.py:23
  18.4 11.8 %collective-permute-start.6 = (bf16[256,768]{1,0:T(8,128)(2,1)S(1)}, bf16[256,768]{1,0:T(8,128)(2,1)S(1)}, u32[]{:S(2)}, u32[]{:S(2)}) collective-permute-start(bf16[256,768]{1,0:T(8,128)(2,1)S(1)} %collective-permute-done.refs_1_), channel_id=1, source_target_pairs={{0,3},{1,0},{2,1},{3,2},{4,7},{5,4},{6,5},{7,6},{8,11},{9,8},{10,9... | collective-permute-start | bytes 1179656 | tf_op jit(solution)/shard_map/ppermute | solution.py:23
  19.1 11.0 %collective-permute-start.5 = (bf16[256,768]{1,0:T(8,128)(2,1)S(1)}, bf16[256,768]{1,0:T(8,128)(2,1)S(1)}, u32[]{:S(2)}, u32[]{:S(2)}) collective-permute-start(bf16[256,768]{1,0:T(8,128)(2,1)S(1)} %collective-permute-done.refs_1_), channel_id=1, source_target_pairs={{0,1},{1,2},{2,3},{3,0},{4,5},{5,6},{6,7},{7,4},{8,9},{9,10},{10,1... | collective-permute-start | bytes 1179656 | tf_op jit(solution)/shard_map/ppermute | solution.py:23
  37.4 23.0 %collective-permute-start.7 = (bf16[256,768]{1,0:T(8,128)(2,1)}, bf16[256,768]{1,0:T(8,128)(2,1)S(1)}, u32[]{:S(2)}, u32[]{:S(2)}) collective-permute-start(bf16[256,768]{1,0:T(8,128)(2,1)} %get-tuple-element.41), channel_id=1, source_target_pairs={{0,32},{32,64},{64,96},{96,0},{1,33},{33,65},{65,97},{97,1},{2,34}... | collective-permute-start | bytes 1179656 | tf_op jit(solution)/shard_map/ppermute | solution.py:23
  39.0 21.4 %collective-permute-start.8 = (bf16[256,768]{1,0:T(8,128)(2,1)}, bf16[256,768]{1,0:T(8,128)(2,1)S(1)}, u32[]{:S(2)}, u32[]{:S(2)}) collective-permute-start(bf16[256,768]{1,0:T(8,128)(2,1)} %get-tuple-element.42), channel_id=1, source_target_pairs={{0,64},{32,96},{64,0},{96,32},{1,65},{33,97},{65,1},{97,33},{2,66}... | collective-permute-start | bytes 1179656 | tf_op jit(solution)/shard_map/ppermute | solution.py:23
  41.7 19.5 %collective-permute-start.10 = (bf16[256,768]{1,0:T(8,128)(2,1)}, bf16[256,768]{1,0:T(8,128)(2,1)S(1)}, u32[]{:S(2)}, u32[]{:S(2)}) collective-permute-start(bf16[256,768]{1,0:T(8,128)(2,1)} %get-tuple-element.44), channel_id=1, source_target_pairs={{0,96},{32,0},{64,32},{96,64},{1,97},{33,1},{65,33},{97,65},{2,98}... | collective-permute-start | bytes 1179656 | tf_op jit(solution)/shard_map/ppermute | solution.py:23
  51.8 28.5 %collective-permute-start.22 = (bf16[256,1536]{1,0:T(8,128)(2,1)S(1)}, bf16[256,1536]{1,0:T(8,128)(2,1)S(1)}, u32[]{:S(2)}, u32[]{:S(2)}) collective-permute-start(bf16[256,1536]{1,0:T(8,128)(2,1)S(1)} %project.1.grad_ref.refs_7_), channel_id=1, source_target_pairs={{0,96},{32,0},{64,32},{96,64},{1,97},{33,1},{65,33},{97,65},{2,98}... | collective-permute-start | bytes 2359304 | tf_op jit(solution)/shard_map/ppermute | solution.py:23
  51.9 28.4 %collective-permute-start.21 = (bf16[256,1536]{1,0:T(8,128)(2,1)S(1)}, bf16[256,1536]{1,0:T(8,128)(2,1)S(1)}, u32[]{:S(2)}, u32[]{:S(2)}) collective-permute-start(bf16[256,1536]{1,0:T(8,128)(2,1)S(1)} %project.1.grad_ref.refs_7_), channel_id=1, source_target_pairs={{0,32},{32,64},{64,96},{96,0},{1,33},{33,65},{65,97},{97,1},{2,34}... | collective-permute-start | bytes 2359304 | tf_op jit(solution)/shard_map/ppermute | solution.py:23
  60.5 23.3 %collective-permute-start.9 = (bf16[384,768]{1,0:T(8,128)(2,1)S(1)}, bf16[384,768]{1,0:T(8,128)(2,1)}, u32[]{:S(2)}, u32[]{:S(2)}) collective-permute-start(bf16[384,768]{1,0:T(8,128)(2,1)S(1)} %pad_maximum_fusion.1), channel_id=1, source_target_pairs={{0,3},{1,0},{2,1},{3,2},{4,7},{5,4},{6,5},{7,6},{8,11},{9,8},{10,9... | collective-permute-start | bytes 1769480 | tf_op jit(solution)/shard_map/ppermute | solution.py:23
  61.3 22.5 %collective-permute-start.11 = (bf16[384,768]{1,0:T(8,128)(2,1)S(1)}, bf16[384,768]{1,0:T(8,128)(2,1)}, u32[]{:S(2)}, u32[]{:S(2)}) collective-permute-start(bf16[384,768]{1,0:T(8,128)(2,1)S(1)} %pad_maximum_fusion.2), channel_id=1, source_target_pairs={{0,1},{1,2},{2,3},{3,0},{4,5},{5,6},{6,7},{7,4},{8,9},{9,10},{10,1... | collective-permute-start | bytes 1769480 | tf_op jit(solution)/shard_map/ppermute | solution.py:23
  76.4 11.0 %collective-permute-start.14 = (bf16[256,768]{1,0:T(8,128)(2,1)}, bf16[256,768]{1,0:T(8,128)(2,1)S(1)}, u32[]{:S(2)}, u32[]{:S(2)}) collective-permute-start(bf16[256,768]{1,0:T(8,128)(2,1)} %get-tuple-element.49), channel_id=1, source_target_pairs={{0,4},{4,0},{1,5},{5,1},{2,6},{6,2},{3,7},{7,3},{8,12},{12,8},{9,1... | collective-permute-start | bytes 1179656 | tf_op jit(solution)/shard_map/ppermute | solution.py:23
  83.8 15.8 %collective-permute-start.17 = (bf16[256,768]{1,0:T(8,128)(2,1)}, bf16[256,768]{1,0:T(8,128)(2,1)S(1)}, u32[]{:S(2)}, u32[]{:S(2)}) collective-permute-start(bf16[256,768]{1,0:T(8,128)(2,1)} %get-tuple-element.54), channel_id=1, source_target_pairs={{0,3},{1,0},{2,1},{3,2},{4,7},{5,4},{6,5},{7,6},{8,11},{9,8},{10,9... | collective-permute-start | bytes 1179656 | tf_op jit(solution)/shard_map/ppermute | solution.py:23
  83.9 15.7 %collective-permute-start.16 = (bf16[256,768]{1,0:T(8,128)(2,1)}, bf16[256,768]{1,0:T(8,128)(2,1)S(1)}, u32[]{:S(2)}, u32[]{:S(2)}) collective-permute-start(bf16[256,768]{1,0:T(8,128)(2,1)} %get-tuple-element.52), channel_id=1, source_target_pairs={{0,1},{1,2},{2,3},{3,0},{4,5},{5,6},{6,7},{7,4},{8,9},{9,10},{10,1... | collective-permute-start | bytes 1179656 | tf_op jit(solution)/shard_map/ppermute | solution.py:23
  99.6 16.9 %collective-permute-start.26 = (bf16[768,768]{1,0:T(8,128)(2,1)}, bf16[768,768]{1,0:T(8,128)(2,1)S(1)}, u32[]{:S(2)}, u32[]{:S(2)}) collective-permute-start(bf16[768,768]{1,0:T(8,128)(2,1)} %get-tuple-element.66), channel_id=1, source_target_pairs={{0,8},{8,0},{1,9},{9,1},{2,10},{10,2},{3,11},{11,3},{4,12},{12,4},... | collective-permute-start | bytes 3538952 | tf_op jit(solution)/shard_map/ppermute | solution.py:23
  99.9 16.4 %collective-permute-start.18 = (bf16[256,768]{1,0:T(8,128)(2,1)S(1)}, bf16[256,768]{1,0:T(8,128)(2,1)S(1)}, u32[]{:S(2)}, u32[]{:S(2)}) collective-permute-start(bf16[256,768]{1,0:T(8,128)(2,1)S(1)} %add_convert_fusion.3), channel_id=1, source_target_pairs={{0,4},{4,0},{1,5},{5,1},{2,6},{6,2},{3,7},{7,3},{8,12},{12,8},{9,1... | collective-permute-start | bytes 1179656 | tf_op jit(solution)/shard_map/ppermute | solution.py:23
  103.2 14.7 %collective-permute-start.15 = (bf16[256,768]{1,0:T(8,128)(2,1)S(1)}, bf16[256,768]{1,0:T(8,128)(2,1)S(1)}, u32[]{:S(2)}, u32[]{:S(2)}) collective-permute-start(bf16[256,768]{1,0:T(8,128)(2,1)S(1)} %add_convert_fusion.4), channel_id=1, source_target_pairs={{0,2},{1,3},{2,0},{3,1},{4,6},{5,7},{6,4},{7,5},{8,10},{9,11},{10,... | collective-permute-start | bytes 1179656 | tf_op jit(solution)/shard_map/ppermute | solution.py:23
  104.5 19.9 %collective-permute-start.13 = (bf16[256,768]{1,0:T(8,128)(2,1)S(1)}, bf16[256,768]{1,0:T(8,128)(2,1)S(1)}, u32[]{:S(2)}, u32[]{:S(2)}) collective-permute-start(bf16[256,768]{1,0:T(8,128)(2,1)S(1)} %copy-done.25), channel_id=1, source_target_pairs={{0,3},{1,0},{2,1},{3,2},{4,7},{5,4},{6,5},{7,6},{8,11},{9,8},{10,9... | collective-permute-start | bytes 1179656 | tf_op jit(solution)/shard_map/ppermute | solution.py:23
  104.5 19.9 %collective-permute-start.12 = (bf16[256,768]{1,0:T(8,128)(2,1)S(1)}, bf16[256,768]{1,0:T(8,128)(2,1)S(1)}, u32[]{:S(2)}, u32[]{:S(2)}) collective-permute-start(bf16[256,768]{1,0:T(8,128)(2,1)S(1)} %copy-done.24), channel_id=1, source_target_pairs={{0,1},{1,2},{2,3},{3,0},{4,5},{5,6},{6,7},{7,4},{8,9},{9,10},{10,1... | collective-permute-start | bytes 1179656 | tf_op jit(solution)/shard_map/ppermute | solution.py:23
  116.3 19.2 %collective-permute-start.25 = (bf16[768,768]{1,0:T(8,128)(2,1)}, bf16[768,768]{1,0:T(8,128)(2,1)S(1)}, u32[]{:S(2)}, u32[]{:S(2)}) collective-permute-start(bf16[768,768]{1,0:T(8,128)(2,1)} %get-tuple-element.64), channel_id=1, source_target_pairs={{0,8},{8,0},{1,9},{9,1},{2,10},{10,2},{3,11},{11,3},{4,12},{12,4},... | collective-permute-start | bytes 3538952 | tf_op jit(solution)/shard_map/ppermute | solution.py:23
  116.7 18.7 %collective-permute-start.27 = (bf16[384,768]{1,0:T(8,128)(2,1)S(1)}, bf16[384,768]{1,0:T(8,128)(2,1)S(1)}, u32[]{:S(2)}, u32[]{:S(2)}) collective-permute-start(bf16[384,768]{1,0:T(8,128)(2,1)S(1)} %add_convert_fusion.1), channel_id=1, source_target_pairs={{0,16},{16,0},{1,17},{17,1},{2,18},{18,2},{3,19},{19,3},{4,20},{20... | collective-permute-start | bytes 1769480 | tf_op jit(solution)/shard_map/ppermute | solution.py:23
  135.7 13.0 %collective-permute-start.29 = (bf16[384,768]{1,0:T(8,128)(2,1)S(1)}, bf16[384,768]{1,0:T(8,128)(2,1)S(1)}, u32[]{:S(2)}, u32[]{:S(2)}) collective-permute-start(bf16[384,768]{1,0:T(8,128)(2,1)S(1)} %add_convert_fusion), channel_id=1, source_target_pairs={{0,16},{16,0},{1,17},{17,1},{2,18},{18,2},{3,19},{19,3},{4,20},{20... | collective-permute-start | bytes 1769480 | tf_op jit(solution)/shard_map/ppermute | solution.py:23
  (38 other events, 261.5 us)
